TPU v7x, 128 devices: a whole 4x4x4 slice. The times are simulated.
128 devices in a mesh: grp: 2 (over core), dev: 64 (over x, y, z).
Axes of the slice: x: 4, y: 4, z: 4, core: 2. Of those that a mesh axis runs over, the one named last changes fastest.
Arguments:
- states: bfloat16 [2048, 3584], P(('grp', 'dev')), may hold values from -6 to 6
- routes: int32 [2048, 8], P(('grp', 'dev')), may hold values from 0 to 127, all different within a row; in each aligned block of 16 rows (0 to 15, 16 to 31, ...) at most 2 rows name the same one
- gate_scores: float32 [2048, 8], P(('grp', 'dev')), may hold values from 0.05 to 1
- w_in: bfloat16 [128, 3584, 2048], P(('grp', 'dev')), may hold values from -0.09375 to 0.09375
- w_out: bfloat16 [128, 1024, 3584], P(('grp', 'dev')), may hold values from -0.1875 to 0.1875
Outputs:
- mixed: bfloat16 [2048, 3584], P(('grp', 'dev'))
Inputs may be any that keep to these rules, and one draw needn't show every extreme that they name: `routes`: each row names 8 different experts; among the rows of one device no expert is named by more than 2 rows, a bound that some block reaches of some device in every draw.
All inputs are finite; a program needn't handle non-finite values.
Results may differ from a plain program's by a relative error of at most 0.0051.
Values may be sent and summed in bfloat16 or wider, within the bound.
No kernel may reach another device: no remote copies, remote signals or barrier semaphores. Data moves between devices by JAX's collectives and lax.ppermute only.
A program may use at most 64 MiB of HBM per device.

v0:
```python
import jax
import jax.numpy as jnp
from jax import lax
from jax.sharding import PartitionSpec as P

route_scale = 2.5


def expert_ffn(inputs, w_first, w_second):
    projected = jnp.dot(inputs, w_first, preferred_element_type=jnp.float32)
    width = w_second.shape[0]
    gate_part = projected[:, :width]
    up_part = projected[:, width:]
    hidden = (jax.nn.silu(gate_part) * up_part).astype(jnp.bfloat16)
    return jnp.dot(hidden, w_second, preferred_element_type=jnp.float32).astype(jnp.bfloat16)


def body(states, routes, gate_scores, w_in, w_out):
    rows, width = states.shape
    top = routes.shape[1]
    experts = lax.axis_size(("grp", "dev"))
    slots = 2 * rows * top // experts
    count = rows * top
    chosen = routes.reshape(-1)
    onehot = (chosen[:, None] == jnp.arange(experts, dtype=jnp.int32)[None, :]).astype(jnp.int32)
    position = jnp.sum(jnp.cumsum(onehot, axis=0) * onehot, axis=1) - 1
    target = chosen * slots + position
    row_ids = jnp.arange(count, dtype=jnp.int32) // top
    outgoing = jnp.zeros((experts * slots, width), jnp.bfloat16).at[target].set(states[row_ids])
    w_first = w_in[0]
    w_second = w_out[0]
    received = lax.all_to_all(
        outgoing.reshape(experts, slots, width),
        ("grp", "dev"),
        split_axis=0,
        concat_axis=0,
        tiled=True,
    )
    number = received.shape[1]
    result = expert_ffn(received.reshape(-1, width), w_first, w_second)
    result = result.reshape(experts, number, width)
    returned = lax.all_to_all(result, ("grp", "dev"), split_axis=0, concat_axis=0, tiled=True)
    gathered = returned.reshape(experts * slots, width)[target]
    weights = gate_scores / jnp.sum(gate_scores, axis=1, keepdims=True) * route_scale
    weighted = weights.reshape(-1)[:, None] * gathered.astype(jnp.float32)
    combined = jnp.sum(weighted.reshape(rows, top, width), axis=1)
    return (states.astype(jnp.float32) + combined).astype(jnp.bfloat16)


def solution(mesh):
    return jax.shard_map(
        body,
        mesh=mesh,
        in_specs=(
            P(("grp", "dev"), None),
            P(("grp", "dev"), None),
            P(("grp", "dev"), None),
            P(("grp", "dev"), None, None),
            P(("grp", "dev"), None, None),
        ),
        out_specs=P(("grp", "dev"), None),
        check_vma=False,
    )
```

profile of v0, /device:TPU:1, one launch (start us, length us, event | category | flops | bytes accessed | tf_op | source)
XLA Modules:
  0.0 108.1 jit_solution(7206864196619252171)
XLA Ops:
  0.0 0.8 copy.11
  0.8 0.7 broadcast_multiply_fusion
  1.5 0.1 eq.15
  1.5 0.1 fusion.14
  1.6 0.2 reduce_window_sum.11
  1.8 0.2 select_reduce_fusion
  2.0 0.1 copy.10
  2.1 0.1 mul.46
  2.2 7.6 %scatter_custom_fusion = bf16[256,3584]{1,0:T(8,128)(2,1)} fusion(s32[128]{0:T(128)S(1)} %fusion.16, bf16[16,3584]{1,0:T(8,128)(2,1)} %param.5, s32[1024]{0:T(1024)S(1)} %pad_clamp_fusion.1, bf16[]{:T(256)} %constant.31.clone.1), kind=kCustom, calls=%fused_computation.12 | custom fusion | bytes 1835520 | tf_op jit(solution)/shard_map/scatter | solution.py:29
  9.8 3.9 %reshape.101 = bf16[128,2,3584]{2,1,0:T(2,128)(2,1)S(1)} reshape(bf16[256,3584]{1,0:T(8,128)(2,1)} %scatter_custom_fusion) | data formatting | bytes 3670016 | tf_op jit(solution)/shard_map/reshape | solution.py:33
  13.7 37.1 %all_to_all.10 = bf16[128,2,3584]{2,1,0:T(2,128)(2,1)} all-to-all(bf16[128,2,3584]{2,1,0:T(2,128)(2,1)S(1)} %reshape.101), channel_id=1, replica_groups=mesh['grp'=2,'dev'=64] {'grp','dev'}, dimensions={0} | all-to-all | bytes 3670016 | tf_op jit(solution)/shard_map/all_to_all | solution.py:32
  50.7 4.1 %reshape.102 = bf16[256,3584]{1,0:T(8,128)(2,1)S(1)} reshape(bf16[128,2,3584]{2,1,0:T(2,128)(2,1)} %all_to_all.10) | data formatting | bytes 3670016 | tf_op jit(solution)/shard_map/reshape | solution.py:40
  54.8 7.5 %fusion = f32[256,2048]{1,0:T(8,128)S(1)} fusion(bf16[256,3584]{1,0:T(8,128)(2,1)S(1)} %reshape.102, bf16[1,3584,2048]{2,1,0:T(8,128)(2,1)} %param.8), kind=kOutput, calls=%fused_computation.3 | convolution fusion | flops 3758096384 | bytes 18612224 | tf_op jit(solution)/shard_map/dot_general | solution.py:10
  62.4 5.2 %fusion.4 = bf16[256,3584]{1,0:T(8,128)(2,1)S(1)} fusion(bf16[1,1024,3584]{2,1,0:T(8,128)(2,1)} %param.9, f32[256,2048]{1,0:T(8,128)S(1)} %fusion), kind=kOutput, calls=%fused_computation.7 | convolution fusion | flops 1881538560 | bytes 11272192 | tf_op jit(solution)/shard_map/dot_general | solution.py:15
  67.5 1.7 %reshape.103 = bf16[128,2,3584]{2,1,0:T(2,128)(2,1)} reshape(bf16[256,3584]{1,0:T(8,128)(2,1)S(1)} %fusion.4) | data formatting | bytes 3670016 | tf_op jit(solution)/shard_map/reshape | solution.py:41
  69.2 0.0 copy-start.1
  69.2 7.0 %all-to-all-start.1 = ((bf16[128,2,3584]{2,1,0:T(2,128)(2,1)}), bf16[128,2,3584]{2,1,0:T(2,128)(2,1)}, u32[]{:S(2)}, u32[]{:S(2)}) async-start(bf16[128,2,3584]{2,1,0:T(2,128)(2,1)} %reshape.103), calls=%async_computation.1 | async-start | bytes 3670016 | tf_op jit(solution)/shard_map/all_to_all | solution.py:42
  76.2 0.0 copy-done.1
  76.3 0.1 copy.9
  76.3 25.2 %all-to-all-done.1 = bf16[128,2,3584]{2,1,0:T(2,128)(2,1)} async-done(((bf16[128,2,3584]{2,1,0:T(2,128)(2,1)}), bf16[128,2,3584]{2,1,0:T(2,128)(2,1)}, u32[]{:S(2)}, u32[]{:S(2)}) %all-to-all-start.1) | async-done | bytes 1835040 | tf_op jit(solution)/shard_map/all_to_all | solution.py:42
  101.6 4.1 %reshape.104 = bf16[256,3584]{1,0:T(8,128)(2,1)S(1)} reshape(bf16[128,2,3584]{2,1,0:T(2,128)(2,1)} %all-to-all-done.1) | data formatting | bytes 3670016 | tf_op jit(solution)/shard_map/reshape | solution.py:43
  105.6 0.0 copy-start
  105.6 1.1 %gather_fusion = bf16[128,3584]{1,0:T(8,128)(2,1)S(1)} fusion(bf16[256,3584]{1,0:T(8,128)(2,1)S(1)} %reshape.104, s32[1024]{0:T(1024)S(1)} %pad_clamp_fusion), kind=kCustom, calls=%fused_computation.1 | custom fusion | bytes 1835520 | tf_op jit(solution)/shard_map/gather | solution.py:43
  106.8 0.7 fusion.7
  107.5 0.0 copy-done
  107.5 0.7 add_convert_fusion
  (6 shorter events, 0.1 us)
Async XLA Ops:
  69.2 7.0 %copy-start.1 = (f32[16,8]{0,1:T(8,128)S(1)}, f32[16,8]{0,1:T(8,128)}, u32[]{:S(2)}) copy-start(f32[16,8]{0,1:T(8,128)} %param.7) | copy-start | bytes 1540
  69.2 32.4 %all-to-all-start.1 = ((bf16[128,2,3584]{2,1,0:T(2,128)(2,1)}), bf16[128,2,3584]{2,1,0:T(2,128)(2,1)}, u32[]{:S(2)}, u32[]{:S(2)}) async-start(bf16[128,2,3584]{2,1,0:T(2,128)(2,1)} %reshape.103), calls=%async_computation.1 | async-start | bytes 3670016 | tf_op jit(solution)/shard_map/all_to_all | solution.py:42
  105.6 1.8 %copy-start = (bf16[16,3584]{1,0:T(8,128)(2,1)S(1)}, bf16[16,3584]{1,0:T(8,128)(2,1)}, u32[]{:S(2)}) copy-start(bf16[16,3584]{1,0:T(8,128)(2,1)} %param.5) | copy-start | bytes 344068
where the time goes:
time: 109 us; the launch traced here: 108 us
  blocking collectives  37.1 us (34%)
  waiting for transfers between devices  25.2 us (23%)
  local copies, waits for them, and re-layouts  23.5 us (22%)
  matrix products  12.7 us (12%)
  starting transfers between devices  7 us (6%)
  other arithmetic  2.53 us (2%)
    all_to_all x1, blocking collectives, body(): lax.all_to_all(outgoing.reshape(experts, slots, width), ('grp', 'dev'), s...  37.1 us
    all_to_all x1, waiting for transfers between devices, body(): lax.all_to_all(result, ('grp', 'dev'), split_axis=0, concat_axis=0, tiled...  25.2 us
    scatter x1, local copies, waits for them, and re-layouts, body(): jnp.zeros((experts * slots, width), jnp.bfloat16).at[target]  7.61 us
    dot_general x1, matrix products, expert_ffn(): projected = jnp.dot(inputs, w_first, preferred_element_type=jnp.float32)  7.54 us
    all_to_all x1, starting transfers between devices, body(): lax.all_to_all(result, ('grp', 'dev'), split_axis=0, concat_axis=0, tiled...  7 us
    dot_general x1, matrix products, expert_ffn(): jnp.dot(hidden, w_second, preferred_element_type=jnp.float32)  5.18 us
    reshape x1, local copies, waits for them, and re-layouts, body(): result = expert_ffn(received.reshape(-1, width), w_first, w_second)  4.06 us
    reshape x1, local copies, waits for them, and re-layouts, body(): gathered = returned.reshape(experts * slots, width)[target]  4.06 us
  transfers between devices with their start and end apart: 1, of which 1 were waited for; matrix products, arithmetic and copies ran while one was open for 0% of the time, Pallas kernels for 0%

commit v1 on v0

v1 whole, which is shorter than its diff:
```python
import functools

import jax
import jax.numpy as jnp
from jax import lax
from jax.experimental import pallas as pl
from jax.experimental.pallas import tpu as pltpu
from jax.sharding import PartitionSpec as P

route_scale = 2.5
axes = ("grp", "dev")
most = 2
parts = 4
lines = most * parts
group = 16


def slot_of(routes, columns):
    rows, top = routes.shape
    column = lax.broadcasted_iota(jnp.int32, (rows, columns), 1)
    expert = column // lines
    named = jnp.zeros((rows, columns), jnp.float32)
    for k in range(top):
        named = named + (routes[:, k : k + 1] == expert).astype(jnp.float32)
    earlier = (
        lax.broadcasted_iota(jnp.int32, (rows, rows), 0)
        > lax.broadcasted_iota(jnp.int32, (rows, rows), 1)
    ).astype(jnp.float32)
    position = jnp.dot(earlier, named, preferred_element_type=jnp.float32)
    slot = (column % most).astype(jnp.float32)
    return expert, (named > 0.5) & (jnp.abs(position - slot) < 0.5), column // most % parts


def dispatch_kernel(routes_ref, states_ref, out_ref):
    rows, width = states_ref.shape
    columns, piece = out_ref.shape
    _, filled, part = slot_of(routes_ref[...], columns)
    pick = jnp.concatenate(
        [(filled & (part == p)).astype(jnp.float32) for p in range(parts)], axis=0
    ).astype(jnp.bfloat16)
    source = jnp.concatenate(
        [states_ref[:, p * piece : (p + 1) * piece] for p in range(parts)], axis=0
    )
    step = 128
    for c in range(0, columns, step):
        block = lax.dot_general(
            pick[:, c : c + step],
            source,
            (((0,), (0,)), ((), ())),
            preferred_element_type=jnp.float32,
        )
        out_ref[c : c + step, :] = block.astype(jnp.bfloat16)


def combine_kernel(routes_ref, scores_ref, states_ref, got_ref, out_ref):
    rows, width = states_ref.shape
    columns, piece = got_ref.shape
    routes = routes_ref[...]
    scores = scores_ref[...]
    weights = scores / jnp.sum(scores, axis=1, keepdims=True) * route_scale
    expert, filled, part = slot_of(routes, columns)
    weight = jnp.zeros((rows, columns), jnp.float32)
    for k in range(routes.shape[1]):
        weight = weight + jnp.where(routes[:, k : k + 1] == expert, weights[:, k : k + 1], 0.0)
    weight = jnp.where(filled, weight, 0.0)
    high = weight.astype(jnp.bfloat16).astype(jnp.float32)
    low = weight - high
    mix = jnp.concatenate(
        [jnp.where(part == p, w, 0.0) for w in (high, low) for p in range(parts)], axis=0
    ).astype(jnp.bfloat16)
    total = jnp.dot(mix, got_ref[...], preferred_element_type=jnp.float32)
    for p in range(parts):
        both = total[p * rows : (p + 1) * rows] + total[(parts + p) * rows : (parts + p + 1) * rows]
        own = states_ref[:, p * piece : (p + 1) * piece].astype(jnp.float32)
        out_ref[:, p * piece : (p + 1) * piece] = (own + both).astype(jnp.bfloat16)


def regroup(inverse):
    size = group * lines
    there = lax.broadcasted_iota(jnp.int32, (size, size), 1 if inverse else 0)
    here = lax.broadcasted_iota(jnp.int32, (size, size), 0 if inverse else 1)
    part = there // (group * most)
    message = there % (group * most) // most
    match = here == message * lines + part * most + there % most
    return match.astype(jnp.float32).astype(jnp.bfloat16)


def ffn_kernel(
    in_ref, first_hbm, second_hbm, out_ref, first, second, rows_in, hidden, rows_out, first_sem, second_sem
):
    chunks, deep, both = first.shape
    half = both // 2
    _, piece = in_ref.shape
    slots = rows_in.shape[1]
    copies = []
    for c in range(chunks):
        for h in range(2):
            copies.append(
                pltpu.make_async_copy(
                    first_hbm.at[0, :, pl.ds(h * half * chunks + c * half, half)],
                    first.at[c, :, pl.ds(h * half, half)],
                    first_sem.at[c, h],
                )
            )
    for p in range(parts):
        copies.append(
            pltpu.make_async_copy(
                second_hbm.at[0, :, pl.ds(p * piece, piece)], second.at[p], second_sem.at[p]
            )
        )
    for copy in copies:
        copy.start()
    size = group * lines
    each = group * most
    order = regroup(False)
    for c in range(in_ref.shape[0] // size):
        block = jnp.dot(order, in_ref[c * size : (c + 1) * size, :], preferred_element_type=jnp.float32)
        block = block.astype(jnp.bfloat16)
        for p in range(parts):
            rows_in[p, c * each : (c + 1) * each, :] = block[p * each : (p + 1) * each]
    for c in range(chunks):
        copies[2 * c].wait()
        copies[2 * c + 1].wait()
        total = jnp.zeros((slots, both), jnp.float32)
        for p in range(parts):
            total = total + jnp.dot(
                rows_in[p], first[c, p * piece : (p + 1) * piece, :], preferred_element_type=jnp.float32
            )
        gate, up = total[:, :half], total[:, half:]
        hidden[:, c * half : (c + 1) * half] = (gate / (1.0 + jnp.exp(-gate)) * up).astype(jnp.bfloat16)
    for p in range(parts):
        copies[2 * chunks + p].wait()
        rows_out[p] = jnp.dot(hidden[...], second[p], preferred_element_type=jnp.float32).astype(
            jnp.bfloat16
        )
    back = regroup(True)
    for c in range(out_ref.shape[0] // size):
        block = jnp.concatenate([rows_out[p, c * each : (c + 1) * each, :] for p in range(parts)], axis=0)
        block = jnp.dot(back, block, preferred_element_type=jnp.float32)
        out_ref[c * size : (c + 1) * size, :] = block.astype(jnp.bfloat16)


def body(states, routes, gate_scores, w_in, w_out):
    rows, width = states.shape
    experts = lax.axis_size(axes)
    piece = width // parts
    columns = experts * lines
    slots = experts * most
    _, deep, both = w_in.shape
    inner = w_out.shape[1]
    chunks = 4
    vmem = pl.BlockSpec(memory_space=pltpu.VMEM)
    hbm = pl.BlockSpec(memory_space=pl.ANY)
    message = jax.ShapeDtypeStruct((columns, piece), jnp.bfloat16)

    outgoing = pl.pallas_call(
        dispatch_kernel,
        out_shape=message,
        in_specs=[vmem] * 2,
        out_specs=vmem,
        compiler_params=pltpu.CompilerParams(vmem_limit_bytes=24 << 20),
        name="dispatch",
    )(routes, states)
    received = lax.all_to_all(outgoing, axes, split_axis=0, concat_axis=0, tiled=True)
    result = pl.pallas_call(
        ffn_kernel,
        out_shape=message,
        in_specs=[vmem, hbm, hbm],
        out_specs=vmem,
        scratch_shapes=[
            pltpu.VMEM((chunks, deep, both // chunks), jnp.bfloat16),
            pltpu.VMEM((parts, inner, piece), jnp.bfloat16),
            pltpu.VMEM((parts, slots, piece), jnp.bfloat16),
            pltpu.VMEM((slots, inner), jnp.bfloat16),
            pltpu.VMEM((parts, slots, piece), jnp.bfloat16),
            pltpu.SemaphoreType.DMA((chunks, 2)),
            pltpu.SemaphoreType.DMA((parts,)),
        ],
        compiler_params=pltpu.CompilerParams(vmem_limit_bytes=48 << 20),
        cost_estimate=pl.CostEstimate(
            flops=2 * slots * width * inner * 3, bytes_accessed=2 * width * inner * 3, transcendentals=slots * inner
        ),
        name="expert_ffn",
    )(received, w_in, w_out)
    returned = lax.all_to_all(result, axes, split_axis=0, concat_axis=0, tiled=True)
    return pl.pallas_call(
        combine_kernel,
        out_shape=jax.ShapeDtypeStruct((rows, width), jnp.bfloat16),
        in_specs=[vmem] * 4,
        out_specs=vmem,
        compiler_params=pltpu.CompilerParams(vmem_limit_bytes=24 << 20),
        name="combine",
    )(routes, gate_scores, states, returned)


def solution(mesh):
    return jax.shard_map(
        body,
        mesh=mesh,
        in_specs=(
            P(axes, None),
            P(axes, None),
            P(axes, None),
            P(axes, None, None),
            P(axes, None, None),
        ),
        out_specs=P(axes, None),
        check_vma=False,
    )
```

time: 109 us -> 87 us (0.80)
  local copies, waits for them, and re-layouts: 23.5 us -> 1.74 us
  Pallas kernels: 0 us -> 15.6 us
  matrix products: 12.7 us -> 0 us
  other arithmetic: 2.53 us -> 0 us
    pallas_call x0 -> x3, Pallas kernels: none -> 15.6 us  [the longest x1 13.4 us: body(): pl.pallas_call(ffn_kernel, out_shape=message, in_specs=[vmem, hbm, hbm],...]
    reshape x4 -> x0, local copies, waits for them, and re-layouts: 13.7 us -> none  [the longest x1 4.06 us: body(): result = expert_ffn(received.reshape(-1, width), w_first, w_second)]
    dot_general x2 -> x0, matrix products: 12.7 us -> none  [the longest x1 7.54 us: expert_ffn(): projected = jnp.dot(inputs, w_first, preferred_element_type=jnp.float32)]
    scatter x1 -> x0, local copies, waits for them, and re-layouts: 7.61 us -> none  [body(): jnp.zeros((experts * slots, width), jnp.bfloat16).at[target]]
    gather x1 -> x0, local copies, waits for them, and re-layouts: 1.11 us -> none  [body(): gathered = returned.reshape(experts * slots, width)[target]]
where the time goes in v1:
time: 87 us; the launch traced here: 86.6 us
  blocking collectives  37 us (43%)
  waiting for transfers between devices  25.6 us (29%)
  Pallas kernels  15.6 us (18%)
  starting transfers between devices  6.61 us (8%)
  local copies, waits for them, and re-layouts  1.74 us (2%)
    all_to_all x1, blocking collectives, body(): lax.all_to_all(outgoing, axes, split_axis=0, concat_axis=0, tiled=True)  37 us
    all_to_all x1, waiting for transfers between devices, body(): lax.all_to_all(result, axes, split_axis=0, concat_axis=0, tiled=True)  25.6 us
    pallas_call x1, Pallas kernels, body(): pl.pallas_call(ffn_kernel, out_shape=message, in_specs=[vmem, hbm, hbm],...  13.4 us
    all_to_all x1, starting transfers between devices, body(): lax.all_to_all(result, axes, split_axis=0, concat_axis=0, tiled=True)  6.61 us
  transfers between devices with their start and end apart: 1, of which 1 were waited for; matrix products, arithmetic and copies ran while one was open for 0% of the time, Pallas kernels for 0%

profile of v1, /device:TPU:1, one launch (start us, length us, event | category | flops | bytes accessed | tf_op | source)
XLA Modules:
  0.0 86.6 jit_solution(14588606526408611351)
XLA Ops:
  0.0 0.8 copy.7.routes_ref
  0.8 0.0 copy-start
  0.8 0.9 %copy-done = bf16[16,3584]{1,0:T(8,128)(2,1)S(1)} copy-done((bf16[16,3584]{1,0:T(8,128)(2,1)S(1)}, bf16[16,3584]{1,0:T(8,128)(2,1)}, u32[]{:S(2)}) %copy-start) | copy-done | bytes 114712
  1.7 0.9 %dispatch.1 = bf16[1024,896]{1,0:T(8,128)(2,1)S(1)} custom-call(s32[16,8]{1,0:T(8,128)S(1)} %copy.7.routes_ref, bf16[16,3584]{1,0:T(8,128)(2,1)S(1)} %copy-done), custom_call_target="tpu_custom_call" | custom-call | tf_op jit(solution)/shard_map/dispatch/pallas_call | solution.py:156
  2.5 37.0 %all_to_all.22 = bf16[128,8,896]{2,1,0:T(8,128)(2,1)S(1)} all-to-all(bf16[128,8,896]{2,1,0:T(8,128)(2,1)S(1)} %bitcast.6), channel_id=1, replica_groups=mesh['grp'=2,'dev'=64] {'grp','dev'}, dimensions={0} | all-to-all | bytes 3670016 | tf_op jit(solution)/shard_map/all_to_all | solution.py:164
  39.5 13.4 %expert_ffn.1 = bf16[1024,896]{1,0:T(8,128)(2,1)} custom-call(bf16[1024,896]{1,0:T(8,128)(2,1)S(1)} %bitcast.4, bf16[1,3584,2048]{2,1,0:T(8,128)(2,1)} %first_hbm.1, bf16[1,1024,3584]{2,1,0:T(8,128)(2,1)} %second_hbm.1), custom_call_target="tpu_custom_call" | custom-call | flops 5637144576 | bytes 22020096 | tf_op jit(solution)/shard_map/expert_ffn/pallas_call | solution.py:165
  52.9 0.0 copy-start.2
  53.0 0.0 copy-start.1
  53.0 6.6 %all-to-all-start.1 = ((bf16[128,8,896]{2,1,0:T(8,128)(2,1)}), bf16[128,8,896]{2,1,0:T(8,128)(2,1)S(1)}, u32[]{:S(2)}, u32[]{:S(2)}) async-start(bf16[128,8,896]{2,1,0:T(8,128)(2,1)} %bitcast.2), calls=%async_computation.1 | async-start | bytes 3670016 | tf_op jit(solution)/shard_map/all_to_all | solution.py:185
  59.6 0.0 copy-done.2
  59.6 0.1 copy.8.scores_ref
  59.7 25.6 %all-to-all-done.1 = bf16[128,8,896]{2,1,0:T(8,128)(2,1)S(1)} async-done(((bf16[128,8,896]{2,1,0:T(8,128)(2,1)}), bf16[128,8,896]{2,1,0:T(8,128)(2,1)S(1)}, u32[]{:S(2)}, u32[]{:S(2)}) %all-to-all-start.1) | async-done | bytes 1835040 | tf_op jit(solution)/shard_map/all_to_all | solution.py:185
  85.2 0.0 copy-done.1
  85.2 1.3 %combine.1 = bf16[16,3584]{1,0:T(8,128)(2,1)} custom-call(s32[16,8]{1,0:T(8,128)S(1)} %copy.7.routes_ref, f32[16,8]{1,0:T(8,128)S(1)} %copy.8.scores_ref, bf16[16,3584]{1,0:T(8,128)(2,1)S(1)} %copy-done.1, bf16[1024,896]{1,0:T(8,128)(2,1)S(1)} %bitcast.5), custom_call_target="tpu_custom_call" | custom-call | tf_op jit(solution)/shard_map/combine/pallas_call | solution.py:186
Async XLA Ops:
  0.8 0.9 %copy-start = (bf16[16,3584]{1,0:T(8,128)(2,1)S(1)}, bf16[16,3584]{1,0:T(8,128)(2,1)}, u32[]{:S(2)}) copy-start(bf16[16,3584]{1,0:T(8,128)(2,1)} %states_ref.3) | copy-start | bytes 344068
  52.9 6.6 %copy-start.2 = (f32[16,8]{0,1:T(8,128)S(1)}, f32[16,8]{0,1:T(8,128)}, u32[]{:S(2)}) copy-start(f32[16,8]{0,1:T(8,128)} %param.7) | copy-start | bytes 1540
  53.0 32.3 %copy-start.1 = (bf16[16,3584]{1,0:T(8,128)(2,1)S(1)}, bf16[16,3584]{1,0:T(8,128)(2,1)}, u32[]{:S(2)}) copy-start(bf16[16,3584]{1,0:T(8,128)(2,1)} %states_ref.3) | copy-start | bytes 344068
  53.0 32.3 %all-to-all-start.1 = ((bf16[128,8,896]{2,1,0:T(8,128)(2,1)}), bf16[128,8,896]{2,1,0:T(8,128)(2,1)S(1)}, u32[]{:S(2)}, u32[]{:S(2)}) async-start(bf16[128,8,896]{2,1,0:T(8,128)(2,1)} %bitcast.2), calls=%async_computation.1 | async-start | bytes 3670016 | tf_op jit(solution)/shard_map/all_to_all | solution.py:185

commit v2 on v1

--- a/solution.py
+++ b/solution.py
@@ -34,7 +34,7 @@
 def dispatch_kernel(routes_ref, states_ref, out_ref):
     rows, width = states_ref.shape
     columns, piece = out_ref.shape
-    _, filled, part = slot_of(routes_ref[...], columns)
+    _, filled, part = slot_of(routes_ref[...].T, columns)
     pick = jnp.concatenate(
         [(filled & (part == p)).astype(jnp.float32) for p in range(parts)], axis=0
     ).astype(jnp.bfloat16)
@@ -55,8 +55,8 @@
 def combine_kernel(routes_ref, scores_ref, states_ref, got_ref, out_ref):
     rows, width = states_ref.shape
     columns, piece = got_ref.shape
-    routes = routes_ref[...]
-    scores = scores_ref[...]
+    routes = routes_ref[...].T
+    scores = scores_ref[...].T
     weights = scores / jnp.sum(scores, axis=1, keepdims=True) * route_scale
     expert, filled, part = slot_of(routes, columns)
     weight = jnp.zeros((rows, columns), jnp.float32)
@@ -85,31 +85,11 @@
     return match.astype(jnp.float32).astype(jnp.bfloat16)
 
 
-def ffn_kernel(
-    in_ref, first_hbm, second_hbm, out_ref, first, second, rows_in, hidden, rows_out, first_sem, second_sem
-):
-    chunks, deep, both = first.shape
-    half = both // 2
+def ffn_kernel(in_ref, first, second, out_ref, rows_in, hidden, rows_out):
+    _, deep, both = first.shape
+    inner = both // 2
     _, piece = in_ref.shape
     slots = rows_in.shape[1]
-    copies = []
-    for c in range(chunks):
-        for h in range(2):
-            copies.append(
-                pltpu.make_async_copy(
-                    first_hbm.at[0, :, pl.ds(h * half * chunks + c * half, half)],
-                    first.at[c, :, pl.ds(h * half, half)],
-                    first_sem.at[c, h],
-                )
-            )
-    for p in range(parts):
-        copies.append(
-            pltpu.make_async_copy(
-                second_hbm.at[0, :, pl.ds(p * piece, piece)], second.at[p], second_sem.at[p]
-            )
-        )
-    for copy in copies:
-        copy.start()
     size = group * lines
     each = group * most
     order = regroup(False)
@@ -118,21 +98,21 @@
         block = block.astype(jnp.bfloat16)
         for p in range(parts):
             rows_in[p, c * each : (c + 1) * each, :] = block[p * each : (p + 1) * each]
-    for c in range(chunks):
-        copies[2 * c].wait()
-        copies[2 * c + 1].wait()
-        total = jnp.zeros((slots, both), jnp.float32)
+    tile = 256
+    for c in range(0, inner, tile):
+        gate = jnp.zeros((slots, tile), jnp.float32)
+        up = jnp.zeros((slots, tile), jnp.float32)
         for p in range(parts):
-            total = total + jnp.dot(
-                rows_in[p], first[c, p * piece : (p + 1) * piece, :], preferred_element_type=jnp.float32
+            deep_part = slice(p * piece, (p + 1) * piece)
+            gate = gate + jnp.dot(rows_in[p], first[0, deep_part, c : c + tile], preferred_element_type=jnp.float32)
+            up = up + jnp.dot(
+                rows_in[p], first[0, deep_part, inner + c : inner + c + tile], preferred_element_type=jnp.float32
             )
-        gate, up = total[:, :half], total[:, half:]
-        hidden[:, c * half : (c + 1) * half] = (gate / (1.0 + jnp.exp(-gate)) * up).astype(jnp.bfloat16)
+        hidden[:, c : c + tile] = (gate / (1.0 + jnp.exp(-gate)) * up).astype(jnp.bfloat16)
     for p in range(parts):
-        copies[2 * chunks + p].wait()
-        rows_out[p] = jnp.dot(hidden[...], second[p], preferred_element_type=jnp.float32).astype(
-            jnp.bfloat16
-        )
+        rows_out[p] = jnp.dot(
+            hidden[...], second[0, :, p * piece : (p + 1) * piece], preferred_element_type=jnp.float32
+        ).astype(jnp.bfloat16)
     back = regroup(True)
     for c in range(out_ref.shape[0] // size):
         block = jnp.concatenate([rows_out[p, c * each : (c + 1) * each, :] for p in range(parts)], axis=0)
@@ -148,9 +128,9 @@
     slots = experts * most
     _, deep, both = w_in.shape
     inner = w_out.shape[1]
-    chunks = 4
+    work = 2 * slots * width * inner * 3
+    weights = 2 * width * inner * 3
     vmem = pl.BlockSpec(memory_space=pltpu.VMEM)
-    hbm = pl.BlockSpec(memory_space=pl.ANY)
     message = jax.ShapeDtypeStruct((columns, piece), jnp.bfloat16)
 
     outgoing = pl.pallas_call(
@@ -158,27 +138,24 @@
         out_shape=message,
         in_specs=[vmem] * 2,
         out_specs=vmem,
-        compiler_params=pltpu.CompilerParams(vmem_limit_bytes=24 << 20),
+        compiler_params=pltpu.CompilerParams(vmem_limit_bytes=8 << 20),
+        cost_estimate=pl.CostEstimate(flops=16 * work, bytes_accessed=8 * weights, transcendentals=0),
         name="dispatch",
-    )(routes, states)
+    )(routes.T, states)
     received = lax.all_to_all(outgoing, axes, split_axis=0, concat_axis=0, tiled=True)
     result = pl.pallas_call(
         ffn_kernel,
         out_shape=message,
-        in_specs=[vmem, hbm, hbm],
+        in_specs=[vmem] * 3,
         out_specs=vmem,
         scratch_shapes=[
-            pltpu.VMEM((chunks, deep, both // chunks), jnp.bfloat16),
-            pltpu.VMEM((parts, inner, piece), jnp.bfloat16),
             pltpu.VMEM((parts, slots, piece), jnp.bfloat16),
             pltpu.VMEM((slots, inner), jnp.bfloat16),
             pltpu.VMEM((parts, slots, piece), jnp.bfloat16),
-            pltpu.SemaphoreType.DMA((chunks, 2)),
-            pltpu.SemaphoreType.DMA((parts,)),
         ],
-        compiler_params=pltpu.CompilerParams(vmem_limit_bytes=48 << 20),
+        compiler_params=pltpu.CompilerParams(vmem_limit_bytes=16 << 20),
         cost_estimate=pl.CostEstimate(
-            flops=2 * slots * width * inner * 3, bytes_accessed=2 * width * inner * 3, transcendentals=slots * inner
+            flops=work, bytes_accessed=weights, transcendentals=slots * inner
         ),
         name="expert_ffn",
     )(received, w_in, w_out)
@@ -190,7 +167,7 @@
         out_specs=vmem,
         compiler_params=pltpu.CompilerParams(vmem_limit_bytes=24 << 20),
         name="combine",
-    )(routes, gate_scores, states, returned)
+    )(routes.T, gate_scores.T, states, returned)
 
 
 def solution(mesh):

time: 87 us -> 81.2 us (0.933)
  blocking collectives: 37 us -> 69 us
  waiting for transfers between devices: 25.6 us -> 0 us
  starting transfers between devices: 6.61 us -> 0 us
  Pallas kernels: 15.6 us -> 10.1 us
    all_to_all x0 -> x1, blocking collectives: none -> 32.1 us  [body(): lax.all_to_all(result, axes, split_axis=0, concat_axis=0, tiled=True)]
    all_to_all x1 -> x0, waiting for transfers between devices: 25.6 us -> none  [body(): lax.all_to_all(result, axes, split_axis=0, concat_axis=0, tiled=True)]
    all_to_all x1 -> x0, starting transfers between devices: 6.61 us -> none  [body(): lax.all_to_all(result, axes, split_axis=0, concat_axis=0, tiled=True)]
    pallas_call x1, Pallas kernels: 13.4 us -> 7.68 us  [body(): pl.pallas_call(ffn_kernel, out_shape=message, in_specs=[vmem] * 3, out_sp...]
  transfers between devices with their start and end apart: 1 -> 0, of which waited for: 1 -> 0; matrix products, arithmetic and copies ran while one was open for 0% -> 0% of each run, Pallas kernels for 0% -> 0%
where the time goes in v2:
time: 81.2 us; the launch traced here: 80.8 us
  blocking collectives  69 us (85%)
  Pallas kernels  10.1 us (12%)
  local copies, waits for them, and re-layouts  1.61 us (2%)
    all_to_all x1, blocking collectives, body(): lax.all_to_all(outgoing, axes, split_axis=0, concat_axis=0, tiled=True)  36.9 us
    all_to_all x1, blocking collectives, body(): lax.all_to_all(result, axes, split_axis=0, concat_axis=0, tiled=True)  32.1 us
    pallas_call x1, Pallas kernels, body(): pl.pallas_call(ffn_kernel, out_shape=message, in_specs=[vmem] * 3, out_sp...  7.68 us

profile of v2, /device:TPU:1, one launch (start us, length us, event | category | flops | bytes accessed | tf_op | source)
XLA Modules:
  0.0 80.8 jit_solution(10729940735413743863)
XLA Ops:
  0.0 0.0 copy-start.2
  0.0 0.9 %copy-done.2 = bf16[16,3584]{1,0:T(8,128)(2,1)S(1)} copy-done((bf16[16,3584]{1,0:T(8,128)(2,1)S(1)}, bf16[16,3584]{1,0:T(8,128)(2,1)}, u32[]{:S(2)}) %copy-start.2) | copy-done | bytes 114712
  0.9 0.0 copy-start.4
  0.9 0.7 copy-done.4
  1.6 0.0 copy-start
  1.6 0.0 copy-start.1
  1.6 1.0 %dispatch.1 = bf16[1024,896]{1,0:T(8,128)(2,1)S(1)} custom-call(s32[8,16]{1,0:T(8,128)S(1)} %bitcast.10, bf16[16,3584]{1,0:T(8,128)(2,1)S(1)} %copy-done.2), custom_call_target="tpu_custom_call" | custom-call | flops 90194313216 | bytes 176160768 | tf_op jit(solution)/shard_map/dispatch/pallas_call | solution.py:136
  2.6 36.9 %all_to_all.22 = bf16[128,8,896]{2,1,0:T(8,128)(2,1)S(1)} all-to-all(bf16[128,8,896]{2,1,0:T(8,128)(2,1)S(1)} %bitcast.9), channel_id=1, replica_groups=mesh['grp'=2,'dev'=64] {'grp','dev'}, dimensions={0} | all-to-all | bytes 3670016 | tf_op jit(solution)/shard_map/all_to_all | solution.py:145
  39.5 0.0 copy-done
  39.5 0.0 copy-done.1
  39.5 7.7 %expert_ffn.1 = bf16[1024,896]{1,0:T(8,128)(2,1)S(1)} custom-call(bf16[1024,896]{1,0:T(8,128)(2,1)S(1)} %bitcast.6, bf16[1,3584,2048]{2,1,0:T(8,128)(2,1)S(1)} %copy-done, bf16[1,1024,3584]{2,1,0:T(8,128)(2,1)S(1)} %copy-done.1), custom_call_target="tpu_custom_call" | custom-call | flops 5637144576 | bytes 22020096 | tf_op jit(solution)/shard_map/expert_ffn/pallas_call | solution.py:146
  47.2 0.0 copy-start.3
  47.2 0.0 copy-start.5
  47.2 0.0 copy-start.6
  47.2 32.1 %all_to_all.23 = bf16[128,8,896]{2,1,0:T(8,128)(2,1)S(1)} all-to-all(bf16[128,8,896]{2,1,0:T(8,128)(2,1)S(1)} %bitcast.7), channel_id=1, replica_groups=mesh['grp'=2,'dev'=64] {'grp','dev'}, dimensions={0} | all-to-all | bytes 3670016 | tf_op jit(solution)/shard_map/all_to_all | solution.py:162
  79.3 0.0 copy-done.3
  79.3 0.0 copy-done.5
  79.3 0.0 copy-done.6
  79.3 1.5 %combine.1 = bf16[16,3584]{1,0:T(8,128)(2,1)} custom-call(s32[8,16]{1,0:T(8,128)S(1)} %bitcast.11, f32[8,16]{1,0:T(8,128)S(1)} %bitcast.12, bf16[16,3584]{1,0:T(8,128)(2,1)S(1)} %copy-done.3, bf16[1024,896]{1,0:T(8,128)(2,1)S(1)} %bitcast.8), custom_call_target="tpu_custom_call" | custom-call | tf_op jit(solution)/shard_map/combine/pallas_call | solution.py:163
Async XLA Ops:
  0.0 0.9 %copy-start.2 = (bf16[16,3584]{1,0:T(8,128)(2,1)S(1)}, bf16[16,3584]{1,0:T(8,128)(2,1)}, u32[]{:S(2)}) copy-start(bf16[16,3584]{1,0:T(8,128)(2,1)} %states_ref.3) | copy-start | bytes 344068
  0.9 0.7 copy-start.4
  1.6 37.9 %copy-start = (bf16[1,3584,2048]{2,1,0:T(8,128)(2,1)S(1)}, bf16[1,3584,2048]{2,1,0:T(8,128)(2,1)}, u32[]{:S(2)}) copy-start(bf16[1,3584,2048]{2,1,0:T(8,128)(2,1)} %first.1) | copy-start | bytes 44040196
  1.6 37.9 %copy-start.1 = (bf16[1,1024,3584]{2,1,0:T(8,128)(2,1)S(1)}, bf16[1,1024,3584]{2,1,0:T(8,128)(2,1)}, u32[]{:S(2)}) copy-start(bf16[1,1024,3584]{2,1,0:T(8,128)(2,1)} %second.1) | copy-start | bytes 22020100
  47.2 32.1 %copy-start.3 = (bf16[16,3584]{1,0:T(8,128)(2,1)S(1)}, bf16[16,3584]{1,0:T(8,128)(2,1)}, u32[]{:S(2)}) copy-start(bf16[16,3584]{1,0:T(8,128)(2,1)} %states_ref.3) | copy-start | bytes 344068
  47.2 32.1 %copy-start.5 = (s32[16,8]{0,1:T(8,128)S(1)}, s32[16,8]{0,1:T(8,128)}, u32[]{:S(2)}) copy-start(s32[16,8]{0,1:T(8,128)} %param.6) | copy-start | bytes 1540
  47.2 32.1 %copy-start.6 = (f32[16,8]{0,1:T(8,128)S(1)}, f32[16,8]{0,1:T(8,128)}, u32[]{:S(2)}) copy-start(f32[16,8]{0,1:T(8,128)} %param.7) | copy-start | bytes 1540

commit v3 on v2

--- a/solution.py
+++ b/solution.py
@@ -31,20 +31,22 @@
     return expert, (named > 0.5) & (jnp.abs(position - slot) < 0.5), column // most % parts
 
 
-def dispatch_kernel(routes_ref, states_ref, out_ref):
-    rows, width = states_ref.shape
-    columns, piece = out_ref.shape
-    _, filled, part = slot_of(routes_ref[...].T, columns)
-    pick = jnp.concatenate(
+def pick_kernel(routes_ref, pick_ref):
+    _, filled, part = slot_of(routes_ref[...].T, pick_ref.shape[1])
+    pick_ref[...] = jnp.concatenate(
         [(filled & (part == p)).astype(jnp.float32) for p in range(parts)], axis=0
     ).astype(jnp.bfloat16)
+
+
+def dispatch_kernel(pick_ref, states_ref, out_ref):
+    columns, piece = out_ref.shape
     source = jnp.concatenate(
         [states_ref[:, p * piece : (p + 1) * piece] for p in range(parts)], axis=0
     )
     step = 128
     for c in range(0, columns, step):
         block = lax.dot_general(
-            pick[:, c : c + step],
+            pick_ref[:, c : c + step],
             source,
             (((0,), (0,)), ((), ())),
             preferred_element_type=jnp.float32,
@@ -86,10 +88,8 @@
 
 
 def ffn_kernel(in_ref, first, second, out_ref, rows_in, hidden, rows_out):
-    _, deep, both = first.shape
-    inner = both // 2
-    _, piece = in_ref.shape
-    slots = rows_in.shape[1]
+    inner, width = second.shape[1:]
+    piece = in_ref.shape[1]
     size = group * lines
     each = group * most
     order = regroup(False)
@@ -97,25 +97,24 @@
         block = jnp.dot(order, in_ref[c * size : (c + 1) * size, :], preferred_element_type=jnp.float32)
         block = block.astype(jnp.bfloat16)
         for p in range(parts):
-            rows_in[p, c * each : (c + 1) * each, :] = block[p * each : (p + 1) * each]
+            rows_in[c * each : (c + 1) * each, p * piece : (p + 1) * piece] = block[p * each : (p + 1) * each]
     tile = 256
     for c in range(0, inner, tile):
-        gate = jnp.zeros((slots, tile), jnp.float32)
-        up = jnp.zeros((slots, tile), jnp.float32)
-        for p in range(parts):
-            deep_part = slice(p * piece, (p + 1) * piece)
-            gate = gate + jnp.dot(rows_in[p], first[0, deep_part, c : c + tile], preferred_element_type=jnp.float32)
-            up = up + jnp.dot(
-                rows_in[p], first[0, deep_part, inner + c : inner + c + tile], preferred_element_type=jnp.float32
-            )
+        gate = jnp.dot(rows_in[...], first[0, :, c : c + tile], preferred_element_type=jnp.float32)
+        up = jnp.dot(
+            rows_in[...], first[0, :, inner + c : inner + c + tile], preferred_element_type=jnp.float32
+        )
         hidden[:, c : c + tile] = (gate / (1.0 + jnp.exp(-gate)) * up).astype(jnp.bfloat16)
-    for p in range(parts):
-        rows_out[p] = jnp.dot(
-            hidden[...], second[0, :, p * piece : (p + 1) * piece], preferred_element_type=jnp.float32
+    tile = 512
+    for c in range(0, width, tile):
+        rows_out[:, c : c + tile] = jnp.dot(
+            hidden[...], second[0, :, c : c + tile], preferred_element_type=jnp.float32
         ).astype(jnp.bfloat16)
     back = regroup(True)
     for c in range(out_ref.shape[0] // size):
-        block = jnp.concatenate([rows_out[p, c * each : (c + 1) * each, :] for p in range(parts)], axis=0)
+        block = jnp.concatenate(
+            [rows_out[c * each : (c + 1) * each, p * piece : (p + 1) * piece] for p in range(parts)], axis=0
+        )
         block = jnp.dot(back, block, preferred_element_type=jnp.float32)
         out_ref[c * size : (c + 1) * size, :] = block.astype(jnp.bfloat16)
 
@@ -133,15 +132,23 @@
     vmem = pl.BlockSpec(memory_space=pltpu.VMEM)
     message = jax.ShapeDtypeStruct((columns, piece), jnp.bfloat16)
 
+    pick = pl.pallas_call(
+        pick_kernel,
+        out_shape=jax.ShapeDtypeStruct((parts * rows, columns), jnp.bfloat16),
+        in_specs=[vmem],
+        out_specs=vmem,
+        compiler_params=pltpu.CompilerParams(vmem_limit_bytes=8 << 20),
+        cost_estimate=pl.CostEstimate(flops=16 * work, bytes_accessed=8 * weights, transcendentals=0),
+        name="pick",
+    )(routes.T)
     outgoing = pl.pallas_call(
         dispatch_kernel,
         out_shape=message,
         in_specs=[vmem] * 2,
         out_specs=vmem,
         compiler_params=pltpu.CompilerParams(vmem_limit_bytes=8 << 20),
-        cost_estimate=pl.CostEstimate(flops=16 * work, bytes_accessed=8 * weights, transcendentals=0),
         name="dispatch",
-    )(routes.T, states)
+    )(pick, states)
     received = lax.all_to_all(outgoing, axes, split_axis=0, concat_axis=0, tiled=True)
     result = pl.pallas_call(
         ffn_kernel,
@@ -149,9 +156,9 @@
         in_specs=[vmem] * 3,
         out_specs=vmem,
         scratch_shapes=[
-            pltpu.VMEM((parts, slots, piece), jnp.bfloat16),
+            pltpu.VMEM((slots, width), jnp.bfloat16),
             pltpu.VMEM((slots, inner), jnp.bfloat16),
-            pltpu.VMEM((parts, slots, piece), jnp.bfloat16),
+            pltpu.VMEM((slots, width), jnp.bfloat16),
         ],
         compiler_params=pltpu.CompilerParams(vmem_limit_bytes=16 << 20),
         cost_estimate=pl.CostEstimate(

time: 81.2 us -> 80.1 us (0.986)
  no operation moved by 1% of the time
where the time goes in v3:
time: 80.1 us; the launch traced here: 79.7 us
  blocking collectives  69 us (86%)
  Pallas kernels  9.33 us (12%)
  local copies, waits for them, and re-layouts  1.28 us (2%)
    all_to_all x1, blocking collectives, body(): lax.all_to_all(outgoing, axes, split_axis=0, concat_axis=0, tiled=True)  37 us
    all_to_all x1, blocking collectives, body(): lax.all_to_all(result, axes, split_axis=0, concat_axis=0, tiled=True)  32.1 us
    pallas_call x1, Pallas kernels, body(): pl.pallas_call(ffn_kernel, out_shape=message, in_specs=[vmem] * 3, out_sp...  6.87 us

profile of v3, /device:TPU:1, one launch (start us, length us, event | category | flops | bytes accessed | tf_op | source)
XLA Modules:
  0.0 79.7 jit_solution(13886249205287700570)
XLA Ops:
  0.0 0.0 copy-start.3
  0.0 0.7 copy-done.3
  0.7 0.0 copy-start.2
  0.7 0.0 copy-start
  0.7 0.0 copy-start.1
  0.7 0.3 pick.1.pick_ref
  1.0 0.6 copy-done.2
  1.6 0.7 dispatch.1
  2.3 37.0 %all_to_all.22 = bf16[128,8,896]{2,1,0:T(8,128)(2,1)S(1)} all-to-all(bf16[128,8,896]{2,1,0:T(8,128)(2,1)S(1)} %bitcast.8), channel_id=1, replica_groups=mesh['grp'=2,'dev'=64] {'grp','dev'}, dimensions={0} | all-to-all | bytes 3670016 | tf_op jit(solution)/shard_map/all_to_all | solution.py:152
  39.2 0.0 copy-done
  39.2 0.0 copy-done.1
  39.2 6.9 %expert_ffn.1 = bf16[1024,896]{1,0:T(8,128)(2,1)S(1)} custom-call(bf16[1024,896]{1,0:T(8,128)(2,1)S(1)} %bitcast.6, bf16[1,3584,2048]{2,1,0:T(8,128)(2,1)S(1)} %copy-done, bf16[1,1024,3584]{2,1,0:T(8,128)(2,1)S(1)} %copy-done.1), custom_call_target="tpu_custom_call" | custom-call | flops 5637144576 | bytes 22020096 | tf_op jit(solution)/shard_map/expert_ffn/pallas_call | solution.py:153
  46.1 0.0 copy-start.4
  46.1 0.0 copy-start.5
  46.1 32.1 %all_to_all.23 = bf16[128,8,896]{2,1,0:T(8,128)(2,1)S(1)} all-to-all(bf16[128,8,896]{2,1,0:T(8,128)(2,1)S(1)} %bitcast.7), channel_id=1, replica_groups=mesh['grp'=2,'dev'=64] {'grp','dev'}, dimensions={0} | all-to-all | bytes 3670016 | tf_op jit(solution)/shard_map/all_to_all | solution.py:169
  78.2 0.0 copy-done.4
  78.2 0.0 copy-done.5
  78.2 1.5 %combine.1 = bf16[16,3584]{1,0:T(8,128)(2,1)} custom-call(s32[8,16]{1,0:T(8,128)S(1)} %bitcast.11, f32[8,16]{1,0:T(8,128)S(1)} %bitcast.12, bf16[16,3584]{1,0:T(8,128)(2,1)S(1)} %copy-done.2, bf16[1024,896]{1,0:T(8,128)(2,1)S(1)} %bitcast.9), custom_call_target="tpu_custom_call" | custom-call | tf_op jit(solution)/shard_map/combine/pallas_call | solution.py:170
Async XLA Ops:
  0.0 0.7 copy-start.3
  0.7 0.9 %copy-start.2 = (bf16[16,3584]{1,0:T(8,128)(2,1)S(1)}, bf16[16,3584]{1,0:T(8,128)(2,1)}, u32[]{:S(2)}) copy-start(bf16[16,3584]{1,0:T(8,128)(2,1)} %states_ref.3) | copy-start | bytes 344068
  0.7 38.5 %copy-start = (bf16[1,3584,2048]{2,1,0:T(8,128)(2,1)S(1)}, bf16[1,3584,2048]{2,1,0:T(8,128)(2,1)}, u32[]{:S(2)}) copy-start(bf16[1,3584,2048]{2,1,0:T(8,128)(2,1)} %first.1) | copy-start | bytes 44040196
  0.7 38.5 %copy-start.1 = (bf16[1,1024,3584]{2,1,0:T(8,128)(2,1)S(1)}, bf16[1,1024,3584]{2,1,0:T(8,128)(2,1)}, u32[]{:S(2)}) copy-start(bf16[1,1024,3584]{2,1,0:T(8,128)(2,1)} %second.1) | copy-start | bytes 22020100
  46.1 32.1 %copy-start.4 = (s32[16,8]{0,1:T(8,128)S(1)}, s32[16,8]{0,1:T(8,128)}, u32[]{:S(2)}) copy-start(s32[16,8]{0,1:T(8,128)} %param.6) | copy-start | bytes 1540
  46.1 32.1 %copy-start.5 = (f32[16,8]{0,1:T(8,128)S(1)}, f32[16,8]{0,1:T(8,128)}, u32[]{:S(2)}) copy-start(f32[16,8]{0,1:T(8,128)} %param.7) | copy-start | bytes 1540

commit v4 on v3

--- a/solution.py
+++ b/solution.py
@@ -1,5 +1,3 @@
-import functools
-
 import jax
 import jax.numpy as jnp
 from jax import lax
@@ -15,11 +13,14 @@
 group = 16
 
 
-def slot_of(routes, columns):
+def column_kernel(expert_ref):
+    expert_ref[...] = lax.broadcasted_iota(jnp.int32, expert_ref.shape, 1) // lines
+
+
+def slot_of(routes, expert):
     rows, top = routes.shape
-    column = lax.broadcasted_iota(jnp.int32, (rows, columns), 1)
-    expert = column // lines
-    named = jnp.zeros((rows, columns), jnp.float32)
+    column = lax.broadcasted_iota(jnp.int32, expert.shape, 1)
+    named = jnp.zeros(expert.shape, jnp.float32)
     for k in range(top):
         named = named + (routes[:, k : k + 1] == expert).astype(jnp.float32)
     earlier = (
@@ -28,11 +29,11 @@
     ).astype(jnp.float32)
     position = jnp.dot(earlier, named, preferred_element_type=jnp.float32)
     slot = (column % most).astype(jnp.float32)
-    return expert, (named > 0.5) & (jnp.abs(position - slot) < 0.5), column // most % parts
+    return (named > 0.5) & (jnp.abs(position - slot) < 0.5), column // most % parts
 
 
-def pick_kernel(routes_ref, pick_ref):
-    _, filled, part = slot_of(routes_ref[...].T, pick_ref.shape[1])
+def pick_kernel(routes_ref, expert_ref, pick_ref):
+    filled, part = slot_of(routes_ref[...].T, expert_ref[...])
     pick_ref[...] = jnp.concatenate(
         [(filled & (part == p)).astype(jnp.float32) for p in range(parts)], axis=0
     ).astype(jnp.bfloat16)
@@ -54,22 +55,20 @@
         out_ref[c : c + step, :] = block.astype(jnp.bfloat16)
 
 
-def combine_kernel(routes_ref, scores_ref, states_ref, got_ref, out_ref):
+def mix_of(routes, scores, pick, expert):
+    weights = scores / jnp.sum(scores, axis=1, keepdims=True) * route_scale
+    weight = jnp.zeros(expert.shape, jnp.float32)
+    for k in range(routes.shape[1]):
+        weight = jnp.where(routes[:, k : k + 1] == expert, weights[:, k : k + 1], weight)
+    high = weight.astype(jnp.bfloat16)
+    low = (weight - high.astype(jnp.float32)).astype(jnp.bfloat16)
+    return jnp.concatenate([pick * jnp.concatenate([w] * parts, axis=0) for w in (high, low)], axis=0)
+
+
+def combine_kernel(routes_ref, scores_ref, pick_ref, expert_ref, states_ref, got_ref, out_ref):
     rows, width = states_ref.shape
     columns, piece = got_ref.shape
-    routes = routes_ref[...].T
-    scores = scores_ref[...].T
-    weights = scores / jnp.sum(scores, axis=1, keepdims=True) * route_scale
-    expert, filled, part = slot_of(routes, columns)
-    weight = jnp.zeros((rows, columns), jnp.float32)
-    for k in range(routes.shape[1]):
-        weight = weight + jnp.where(routes[:, k : k + 1] == expert, weights[:, k : k + 1], 0.0)
-    weight = jnp.where(filled, weight, 0.0)
-    high = weight.astype(jnp.bfloat16).astype(jnp.float32)
-    low = weight - high
-    mix = jnp.concatenate(
-        [jnp.where(part == p, w, 0.0) for w in (high, low) for p in range(parts)], axis=0
-    ).astype(jnp.bfloat16)
+    mix = mix_of(routes_ref[...].T, scores_ref[...].T, pick_ref[...], expert_ref[...])
     total = jnp.dot(mix, got_ref[...], preferred_element_type=jnp.float32)
     for p in range(parts):
         both = total[p * rows : (p + 1) * rows] + total[(parts + p) * rows : (parts + p + 1) * rows]
@@ -125,28 +124,35 @@
     piece = width // parts
     columns = experts * lines
     slots = experts * most
-    _, deep, both = w_in.shape
     inner = w_out.shape[1]
     work = 2 * slots * width * inner * 3
     weights = 2 * width * inner * 3
     vmem = pl.BlockSpec(memory_space=pltpu.VMEM)
     message = jax.ShapeDtypeStruct((columns, piece), jnp.bfloat16)
+    small = pltpu.CompilerParams(vmem_limit_bytes=8 << 20)
 
+    expert = pl.pallas_call(
+        column_kernel,
+        out_shape=jax.ShapeDtypeStruct((rows, columns), jnp.int32),
+        out_specs=vmem,
+        compiler_params=small,
+        cost_estimate=pl.CostEstimate(flops=16 * work, bytes_accessed=8 * weights, transcendentals=0),
+        name="columns",
+    )()
     pick = pl.pallas_call(
         pick_kernel,
         out_shape=jax.ShapeDtypeStruct((parts * rows, columns), jnp.bfloat16),
-        in_specs=[vmem],
+        in_specs=[vmem] * 2,
         out_specs=vmem,
-        compiler_params=pltpu.CompilerParams(vmem_limit_bytes=8 << 20),
-        cost_estimate=pl.CostEstimate(flops=16 * work, bytes_accessed=8 * weights, transcendentals=0),
+        compiler_params=small,
         name="pick",
-    )(routes.T)
+    )(routes.T, expert)
     outgoing = pl.pallas_call(
         dispatch_kernel,
         out_shape=message,
         in_specs=[vmem] * 2,
         out_specs=vmem,
-        compiler_params=pltpu.CompilerParams(vmem_limit_bytes=8 << 20),
+        compiler_params=small,
         name="dispatch",
     )(pick, states)
     received = lax.all_to_all(outgoing, axes, split_axis=0, concat_axis=0, tiled=True)
@@ -170,11 +176,11 @@
     return pl.pallas_call(
         combine_kernel,
         out_shape=jax.ShapeDtypeStruct((rows, width), jnp.bfloat16),
-        in_specs=[vmem] * 4,
+        in_specs=[vmem] * 6,
         out_specs=vmem,
-        compiler_params=pltpu.CompilerParams(vmem_limit_bytes=24 << 20),
+        compiler_params=small,
         name="combine",
-    )(routes.T, gate_scores.T, states, returned)
+    )(routes.T, gate_scores.T, pick, expert, states, returned)
 
 
 def solution(mesh):

time: 80.1 us -> 79.3 us (0.990)
  no operation moved by 1% of the time
where the time goes in v4:
time: 79.3 us; the launch traced here: 79 us
  blocking collectives  69 us (87%)
  Pallas kernels  9.2 us (12%)
    all_to_all x1, blocking collectives, body(): lax.all_to_all(outgoing, axes, split_axis=0, concat_axis=0, tiled=True)  37 us
    all_to_all x1, blocking collectives, body(): lax.all_to_all(result, axes, split_axis=0, concat_axis=0, tiled=True)  32.1 us
    pallas_call x1, Pallas kernels, body(): pl.pallas_call(ffn_kernel, out_shape=message, in_specs=[vmem] * 3, out_sp...  6.88 us

profile of v4, /device:TPU:1, one launch (start us, length us, event | category | flops | bytes accessed | tf_op | source)
XLA Modules:
  0.0 79.0 jit_solution(5996954778057679614)
XLA Ops:
  0.0 0.0 copy-start.3
  0.0 0.0 copy-start.2
  0.0 0.0 copy-start
  0.0 0.0 copy-start.1
  0.0 0.7 copy-done.3
  0.7 0.3 pick.1.pick_ref
  1.0 0.0 copy-done.2
  1.0 0.7 dispatch.1
  1.7 37.0 %all_to_all.22 = bf16[128,8,896]{2,1,0:T(8,128)(2,1)S(1)} all-to-all(bf16[128,8,896]{2,1,0:T(8,128)(2,1)S(1)} %bitcast.9), channel_id=1, replica_groups=mesh['grp'=2,'dev'=64] {'grp','dev'}, dimensions={0} | all-to-all | bytes 3670016 | tf_op jit(solution)/shard_map/all_to_all | solution.py:158
  38.6 0.0 copy-done
  38.6 0.0 copy-done.1
  38.6 6.9 %expert_ffn.1 = bf16[1024,896]{1,0:T(8,128)(2,1)S(1)} custom-call(bf16[1024,896]{1,0:T(8,128)(2,1)S(1)} %bitcast.6, bf16[1,3584,2048]{2,1,0:T(8,128)(2,1)S(1)} %copy-done, bf16[1,1024,3584]{2,1,0:T(8,128)(2,1)S(1)} %copy-done.1), custom_call_target="tpu_custom_call" | custom-call | flops 5637144576 | bytes 22020096 | tf_op jit(solution)/shard_map/expert_ffn/pallas_call | solution.py:159
  45.5 0.0 copy-start.4
  45.5 32.1 %all_to_all.23 = bf16[128,8,896]{2,1,0:T(8,128)(2,1)S(1)} all-to-all(bf16[128,8,896]{2,1,0:T(8,128)(2,1)S(1)} %bitcast.7), channel_id=1, replica_groups=mesh['grp'=2,'dev'=64] {'grp','dev'}, dimensions={0} | all-to-all | bytes 3670016 | tf_op jit(solution)/shard_map/all_to_all | solution.py:175
  77.6 0.0 copy-done.4
  77.6 1.3 %combine.1 = bf16[16,3584]{1,0:T(8,128)(2,1)} custom-call(s32[8,16]{1,0:T(8,128)S(1)} %bitcast.11, f32[8,16]{1,0:T(8,128)S(1)} %bitcast.12, bf16[64,1024]{1,0:T(8,128)(2,1)S(1)} %pick.1.pick_ref, s32[16,1024]{1,0:T(8,128)S(1)} %columns.1.expert_ref, bf16[16,3584]{1,0:T(8,128)(2,1)S(1)} %copy-done.2, bf16[1024,896]{1,0:T(8,128)(2,1)S(1)} %bitcast.8), custom_call_target="tpu_custom_call" | custom-call | tf_op jit(solution)/shard_map/combine/pallas_call | solution.py:176
  (1 shorter events, 0.0 us)
Async XLA Ops:
  0.0 0.7 copy-start.3
  0.0 1.0 %copy-start.2 = (bf16[16,3584]{1,0:T(8,128)(2,1)S(1)}, bf16[16,3584]{1,0:T(8,128)(2,1)}, u32[]{:S(2)}) copy-start(bf16[16,3584]{1,0:T(8,128)(2,1)} %states_ref.3) | copy-start | bytes 344068
  0.0 38.6 %copy-start = (bf16[1,3584,2048]{2,1,0:T(8,128)(2,1)S(1)}, bf16[1,3584,2048]{2,1,0:T(8,128)(2,1)}, u32[]{:S(2)}) copy-start(bf16[1,3584,2048]{2,1,0:T(8,128)(2,1)} %first.1) | copy-start | bytes 44040196
  0.0 38.6 %copy-start.1 = (bf16[1,1024,3584]{2,1,0:T(8,128)(2,1)S(1)}, bf16[1,1024,3584]{2,1,0:T(8,128)(2,1)}, u32[]{:S(2)}) copy-start(bf16[1,1024,3584]{2,1,0:T(8,128)(2,1)} %second.1) | copy-start | bytes 22020100
  45.5 32.1 %copy-start.4 = (f32[16,8]{0,1:T(8,128)S(1)}, f32[16,8]{0,1:T(8,128)}, u32[]{:S(2)}) copy-start(f32[16,8]{0,1:T(8,128)} %param.7) | copy-start | bytes 1540

commit v5 on v4

v5 whole, which is shorter than its diff:
```python
import jax
import jax.numpy as jnp
from jax import lax
from jax.experimental import pallas as pl
from jax.experimental.pallas import tpu as pltpu
from jax.sharding import PartitionSpec as P

route_scale = 2.5
axes = ("grp", "dev")
most = 2


def column_kernel(expert_ref):
    expert_ref[...] = lax.broadcasted_iota(jnp.int32, expert_ref.shape, 1) // most


def pick_kernel(routes_ref, expert_ref, pick_ref):
    routes = routes_ref[...].T
    expert = expert_ref[...]
    rows, top = routes.shape
    named = jnp.zeros(expert.shape, jnp.float32)
    for k in range(top):
        named = named + (routes[:, k : k + 1] == expert).astype(jnp.float32)
    earlier = (
        lax.broadcasted_iota(jnp.int32, (rows, rows), 0)
        > lax.broadcasted_iota(jnp.int32, (rows, rows), 1)
    ).astype(jnp.float32)
    position = jnp.dot(earlier, named, preferred_element_type=jnp.float32)
    slot = (lax.broadcasted_iota(jnp.int32, expert.shape, 1) % most).astype(jnp.float32)
    filled = (named > 0.5) & (jnp.abs(position - slot) < 0.5)
    pick_ref[...] = filled.astype(jnp.float32).astype(jnp.bfloat16)


def dispatch_kernel(pick_ref, states_ref, out_ref):
    experts, _, width = out_ref.shape
    tile = 512
    for c in range(0, width, tile):
        block = lax.dot_general(
            pick_ref[...],
            states_ref[:, c : c + tile],
            (((0,), (0,)), ((), ())),
            preferred_element_type=jnp.float32,
        )
        out_ref[:, :, c : c + tile] = block.astype(jnp.bfloat16).reshape(experts, most, tile)


def ffn_kernel(in_ref, first, second, out_ref, rows_in, hidden):
    inner, width = second.shape[1:]
    rows_in[...] = in_ref[...].reshape(rows_in.shape)
    tile = 256
    for c in range(0, inner, tile):
        gate = jnp.dot(rows_in[...], first[0, :, c : c + tile], preferred_element_type=jnp.float32)
        up = jnp.dot(
            rows_in[...], first[0, :, inner + c : inner + c + tile], preferred_element_type=jnp.float32
        )
        hidden[:, c : c + tile] = (gate / (1.0 + jnp.exp(-gate)) * up).astype(jnp.bfloat16)
    tile = 512
    for c in range(0, width, tile):
        block = jnp.dot(hidden[...], second[0, :, c : c + tile], preferred_element_type=jnp.float32)
        out_ref[:, :, c : c + tile] = block.astype(jnp.bfloat16).reshape(-1, most, tile)


def combine_kernel(routes_ref, scores_ref, pick_ref, expert_ref, states_ref, got_ref, out_ref):
    rows, width = states_ref.shape
    routes = routes_ref[...].T
    scores = scores_ref[...].T
    expert = expert_ref[...]
    pick = pick_ref[...]
    weights = scores / jnp.sum(scores, axis=1, keepdims=True) * route_scale
    weight = jnp.zeros(expert.shape, jnp.float32)
    for k in range(routes.shape[1]):
        weight = jnp.where(routes[:, k : k + 1] == expert, weights[:, k : k + 1], weight)
    high = weight.astype(jnp.bfloat16)
    low = (weight - high.astype(jnp.float32)).astype(jnp.bfloat16)
    mix = jnp.concatenate([pick * high, pick * low], axis=0)
    total = jnp.dot(mix, got_ref[...].reshape(-1, width), preferred_element_type=jnp.float32)
    out_ref[...] = (states_ref[...].astype(jnp.float32) + (total[:rows] + total[rows:])).astype(jnp.bfloat16)


def body(states, routes, gate_scores, w_in, w_out):
    rows, width = states.shape
    experts = lax.axis_size(axes)
    slots = experts * most
    inner = w_out.shape[1]
    work = 2 * slots * width * inner * 3
    weights = 2 * width * inner * 3
    vmem = pl.BlockSpec(memory_space=pltpu.VMEM)
    message = jax.ShapeDtypeStruct((experts, most, width), jnp.bfloat16)
    small = pltpu.CompilerParams(vmem_limit_bytes=8 << 20)

    expert = pl.pallas_call(
        column_kernel,
        out_shape=jax.ShapeDtypeStruct((rows, slots), jnp.int32),
        out_specs=vmem,
        compiler_params=small,
        cost_estimate=pl.CostEstimate(flops=16 * work, bytes_accessed=8 * weights, transcendentals=0),
        name="columns",
    )()
    pick = pl.pallas_call(
        pick_kernel,
        out_shape=jax.ShapeDtypeStruct((rows, slots), jnp.bfloat16),
        in_specs=[vmem] * 2,
        out_specs=vmem,
        compiler_params=small,
        name="pick",
    )(routes.T, expert)
    outgoing = pl.pallas_call(
        dispatch_kernel,
        out_shape=message,
        in_specs=[vmem] * 2,
        out_specs=vmem,
        compiler_params=small,
        name="dispatch",
    )(pick, states)
    received = lax.all_to_all(outgoing, axes, split_axis=0, concat_axis=0, tiled=True)
    result = pl.pallas_call(
        ffn_kernel,
        out_shape=message,
        in_specs=[vmem] * 3,
        out_specs=vmem,
        scratch_shapes=[
            pltpu.VMEM((slots, width), jnp.bfloat16),
            pltpu.VMEM((slots, inner), jnp.bfloat16),
        ],
        compiler_params=pltpu.CompilerParams(vmem_limit_bytes=16 << 20),
        cost_estimate=pl.CostEstimate(
            flops=work, bytes_accessed=weights, transcendentals=slots * inner
        ),
        name="expert_ffn",
    )(received, w_in, w_out)
    returned = lax.all_to_all(result, axes, split_axis=0, concat_axis=0, tiled=True)
    return pl.pallas_call(
        combine_kernel,
        out_shape=jax.ShapeDtypeStruct((rows, width), jnp.bfloat16),
        in_specs=[vmem] * 6,
        out_specs=vmem,
        compiler_params=small,
        name="combine",
    )(routes.T, gate_scores.T, pick, expert, states, returned)


def solution(mesh):
    return jax.shard_map(
        body,
        mesh=mesh,
        in_specs=(
            P(axes, None),
            P(axes, None),
            P(axes, None),
            P(axes, None, None),
            P(axes, None, None),
        ),
        out_specs=P(axes, None),
        check_vma=False,
    )
```

time: 79.3 us -> 78.3 us (0.987)
  Pallas kernels: 9.2 us -> 8.15 us
    pallas_call x1, Pallas kernels: 6.88 us -> 5.9 us  [body(): pl.pallas_call(ffn_kernel, out_shape=message, in_specs=[vmem] * 3, out_sp...]
where the time goes in v5:
time: 78.3 us; the launch traced here: 77.9 us
  blocking collectives  69 us (88%)
  Pallas kernels  8.15 us (10%)
    all_to_all x1, blocking collectives, body(): lax.all_to_all(outgoing, axes, split_axis=0, concat_axis=0, tiled=True)  37 us
    all_to_all x1, blocking collectives, body(): lax.all_to_all(result, axes, split_axis=0, concat_axis=0, tiled=True)  32.1 us
    pallas_call x1, Pallas kernels, body(): pl.pallas_call(ffn_kernel, out_shape=message, in_specs=[vmem] * 3, out_sp...  5.9 us

profile of v5, /device:TPU:1, one launch (start us, length us, event | category | flops | bytes accessed | tf_op | source)
XLA Modules:
  0.0 77.9 jit_solution(16437154689326766492)
XLA Ops:
  0.0 0.0 copy-start.3
  0.0 0.0 copy-start.2
  0.0 0.0 copy-start
  0.0 0.0 copy-start.1
  0.0 0.7 copy-done.3
  0.7 0.3 pick.1.pick_ref
  1.0 0.0 copy-done.2
  1.0 0.7 dispatch.1
  1.7 37.0 %all_to_all.10.in_ref = bf16[128,2,3584]{2,1,0:T(2,128)(2,1)S(1)} all-to-all(bf16[128,2,3584]{2,1,0:T(2,128)(2,1)S(1)} %dispatch.1), channel_id=1, replica_groups=mesh['grp'=2,'dev'=64] {'grp','dev'}, dimensions={0} | all-to-all | bytes 3670016 | tf_op jit(solution)/shard_map/all_to_all | solution.py:115
  38.6 0.0 copy-done
  38.6 0.0 copy-done.1
  38.6 5.9 %expert_ffn.1 = bf16[128,2,3584]{2,1,0:T(2,128)(2,1)S(1)} custom-call(bf16[128,2,3584]{2,1,0:T(2,128)(2,1)S(1)} %all_to_all.10.in_ref, bf16[1,3584,2048]{2,1,0:T(8,128)(2,1)S(1)} %copy-done, bf16[1,1024,3584]{2,1,0:T(8,128)(2,1)S(1)} %copy-done.1), custom_call_target="tpu_custom_call" | custom-call | flops 5637144576 | bytes 22020096 | tf_op jit(solution)/shard_map/expert_ffn/pallas_call | solution.py:116
  44.5 0.0 copy-start.4
  44.5 32.1 %all_to_all.11.got_ref = bf16[128,2,3584]{2,1,0:T(2,128)(2,1)S(1)} all-to-all(bf16[128,2,3584]{2,1,0:T(2,128)(2,1)S(1)} %expert_ffn.1), channel_id=1, replica_groups=mesh['grp'=2,'dev'=64] {'grp','dev'}, dimensions={0} | all-to-all | bytes 3670016 | tf_op jit(solution)/shard_map/all_to_all | solution.py:131
  76.6 0.0 copy-done.4
  76.6 1.3 %combine.1 = bf16[16,3584]{1,0:T(8,128)(2,1)} custom-call(s32[8,16]{1,0:T(8,128)S(1)} %bitcast.3, f32[8,16]{1,0:T(8,128)S(1)} %bitcast.4, bf16[16,256]{1,0:T(8,128)(2,1)S(1)} %pick.1.pick_ref, s32[16,256]{1,0:T(8,128)S(1)} %columns.1.expert_ref, bf16[16,3584]{1,0:T(8,128)(2,1)S(1)} %copy-done.2, bf16[128,2,3584]{2,1,0:T(2,128)(2,1)S(1)} %all_to_all.11.got_ref), custom_call_target="tpu_custom_call" | custom-call | tf_op jit(solution)/shard_map/combine/pallas_call | solution.py:132
  (1 shorter events, 0.0 us)
Async XLA Ops:
  0.0 0.7 copy-start.3
  0.0 1.0 %copy-start.2 = (bf16[16,3584]{1,0:T(8,128)(2,1)S(1)}, bf16[16,3584]{1,0:T(8,128)(2,1)}, u32[]{:S(2)}) copy-start(bf16[16,3584]{1,0:T(8,128)(2,1)} %states_ref.3) | copy-start | bytes 344068
  0.0 38.6 %copy-start = (bf16[1,3584,2048]{2,1,0:T(8,128)(2,1)S(1)}, bf16[1,3584,2048]{2,1,0:T(8,128)(2,1)}, u32[]{:S(2)}) copy-start(bf16[1,3584,2048]{2,1,0:T(8,128)(2,1)} %first.1) | copy-start | bytes 44040196
  0.0 38.6 %copy-start.1 = (bf16[1,1024,3584]{2,1,0:T(8,128)(2,1)S(1)}, bf16[1,1024,3584]{2,1,0:T(8,128)(2,1)}, u32[]{:S(2)}) copy-start(bf16[1,1024,3584]{2,1,0:T(8,128)(2,1)} %second.1) | copy-start | bytes 22020100
  44.5 32.1 %copy-start.4 = (f32[16,8]{0,1:T(8,128)S(1)}, f32[16,8]{0,1:T(8,128)}, u32[]{:S(2)}) copy-start(f32[16,8]{0,1:T(8,128)} %param.7) | copy-start | bytes 1540

commit v6 on v5

--- a/solution.py
+++ b/solution.py
@@ -1,17 +1,29 @@
+import functools
+
 import jax
 import jax.numpy as jnp
 from jax import lax
 from jax.experimental import pallas as pl
 from jax.experimental.pallas import tpu as pltpu
+from jax.sharding import Mesh
 from jax.sharding import PartitionSpec as P
 
 route_scale = 2.5
-axes = ("grp", "dev")
+axes = ("grp", "x", "y", "z")
+turn = ("grp", "z", "y", "x")
 most = 2
 
 
-def column_kernel(expert_ref):
-    expert_ref[...] = lax.broadcasted_iota(jnp.int32, expert_ref.shape, 1) // most
+def column_kernel(sizes, expert_ref):
+    left = lax.broadcasted_iota(jnp.int32, expert_ref.shape, 1) // most
+    place = {}
+    for axis in reversed(turn):
+        place[axis] = left % sizes[axis]
+        left = left // sizes[axis]
+    expert = jnp.zeros_like(left)
+    for axis in axes:
+        expert = expert * sizes[axis] + place[axis]
+    expert_ref[...] = expert
 
 
 def pick_kernel(routes_ref, expert_ref, pick_ref):
@@ -89,7 +101,7 @@
     small = pltpu.CompilerParams(vmem_limit_bytes=8 << 20)
 
     expert = pl.pallas_call(
-        column_kernel,
+        functools.partial(column_kernel, {axis: lax.axis_size(axis) for axis in axes}),
         out_shape=jax.ShapeDtypeStruct((rows, slots), jnp.int32),
         out_specs=vmem,
         compiler_params=small,
@@ -112,7 +124,7 @@
         compiler_params=small,
         name="dispatch",
     )(pick, states)
-    received = lax.all_to_all(outgoing, axes, split_axis=0, concat_axis=0, tiled=True)
+    received = lax.all_to_all(outgoing, turn, split_axis=0, concat_axis=0, tiled=True)
     result = pl.pallas_call(
         ffn_kernel,
         out_shape=message,
@@ -128,7 +140,7 @@
         ),
         name="expert_ffn",
     )(received, w_in, w_out)
-    returned = lax.all_to_all(result, axes, split_axis=0, concat_axis=0, tiled=True)
+    returned = lax.all_to_all(result, turn, split_axis=0, concat_axis=0, tiled=True)
     return pl.pallas_call(
         combine_kernel,
         out_shape=jax.ShapeDtypeStruct((rows, width), jnp.bfloat16),
@@ -140,9 +152,11 @@
 
 
 def solution(mesh):
+    cores, chips = mesh.devices.shape
+    side = round(chips ** (1 / 3))
     return jax.shard_map(
         body,
-        mesh=mesh,
+        mesh=Mesh(mesh.devices.reshape(cores, side, side, side), axes),
         in_specs=(
             P(axes, None),
             P(axes, None),

time: 78.3 us -> 77.9 us (level)
  no operation moved by 1% of the time
where the time goes in v6:
time: 77.9 us; the launch traced here: 77.7 us
  blocking collectives  68.9 us (88%)
  Pallas kernels  8.18 us (11%)
    all_to_all x1, blocking collectives, body(): lax.all_to_all(outgoing, turn, split_axis=0, concat_axis=0, tiled=True)  37.3 us
    all_to_all x1, blocking collectives, body(): lax.all_to_all(result, turn, split_axis=0, concat_axis=0, tiled=True)  31.6 us
    pallas_call x1, Pallas kernels, body(): pl.pallas_call(ffn_kernel, out_shape=message, in_specs=[vmem] * 3, out_sp...  5.9 us

profile of v6, /device:TPU:1, one launch (start us, length us, event | category | flops | bytes accessed | tf_op | source)
XLA Modules:
  0.0 77.7 jit_solution(4910791470693322485)
XLA Ops:
  0.0 0.0 copy-start.3
  0.0 0.0 copy-start.2
  0.0 0.0 copy-start
  0.0 0.0 copy-start.1
  0.1 0.6 copy-done.3
  0.7 0.3 pick.1.pick_ref
  1.0 0.0 copy-done.2
  1.0 0.7 dispatch.1
  1.7 37.3 %all_to_all.10.in_ref = bf16[128,2,3584]{2,1,0:T(2,128)(2,1)S(1)} all-to-all(bf16[128,2,3584]{2,1,0:T(2,128)(2,1)S(1)} %dispatch.1), channel_id=1, replica_groups=mesh['grp'=2,'x'=4,'y'=4,'z'=4] {'grp','z','y','x'}, dimensions={0} | all-to-all | bytes 3670016 | tf_op jit(solution)/shard_map/all_to_all | solution.py:127
  38.9 0.0 copy-done
  38.9 0.0 copy-done.1
  38.9 5.9 %expert_ffn.1 = bf16[128,2,3584]{2,1,0:T(2,128)(2,1)S(1)} custom-call(bf16[128,2,3584]{2,1,0:T(2,128)(2,1)S(1)} %all_to_all.10.in_ref, bf16[1,3584,2048]{2,1,0:T(8,128)(2,1)S(1)} %copy-done, bf16[1,1024,3584]{2,1,0:T(8,128)(2,1)S(1)} %copy-done.1), custom_call_target="tpu_custom_call" | custom-call | flops 5637144576 | bytes 22020096 | tf_op jit(solution)/shard_map/expert_ffn/pallas_call | solution.py:128
  44.8 0.0 copy-start.4
  44.8 31.6 %all_to_all.11.got_ref = bf16[128,2,3584]{2,1,0:T(2,128)(2,1)S(1)} all-to-all(bf16[128,2,3584]{2,1,0:T(2,128)(2,1)S(1)} %expert_ffn.1), channel_id=1, replica_groups=mesh['grp'=2,'x'=4,'y'=4,'z'=4] {'grp','z','y','x'}, dimensions={0} | all-to-all | bytes 3670016 | tf_op jit(solution)/shard_map/all_to_all | solution.py:143
  76.4 0.0 copy-done.4
  76.4 1.3 %combine.1 = bf16[16,3584]{1,0:T(8,128)(2,1)} custom-call(s32[8,16]{1,0:T(8,128)S(1)} %bitcast.3, f32[8,16]{1,0:T(8,128)S(1)} %bitcast.4, bf16[16,256]{1,0:T(8,128)(2,1)S(1)} %pick.1.pick_ref, s32[16,256]{1,0:T(8,128)S(1)} %columns.1.expert_ref, bf16[16,3584]{1,0:T(8,128)(2,1)S(1)} %copy-done.2, bf16[128,2,3584]{2,1,0:T(2,128)(2,1)S(1)} %all_to_all.11.got_ref), custom_call_target="tpu_custom_call" | custom-call | tf_op jit(solution)/shard_map/combine/pallas_call | solution.py:144
  (1 shorter events, 0.0 us)
Async XLA Ops:
  0.0 0.7 copy-start.3
  0.0 1.0 %copy-start.2 = (bf16[16,3584]{1,0:T(8,128)(2,1)S(1)}, bf16[16,3584]{1,0:T(8,128)(2,1)}, u32[]{:S(2)}) copy-start(bf16[16,3584]{1,0:T(8,128)(2,1)} %states_ref.3) | copy-start | bytes 344068
  0.0 38.9 %copy-start = (bf16[1,3584,2048]{2,1,0:T(8,128)(2,1)S(1)}, bf16[1,3584,2048]{2,1,0:T(8,128)(2,1)}, u32[]{:S(2)}) copy-start(bf16[1,3584,2048]{2,1,0:T(8,128)(2,1)} %first.1) | copy-start | bytes 44040196
  0.0 38.9 %copy-start.1 = (bf16[1,1024,3584]{2,1,0:T(8,128)(2,1)S(1)}, bf16[1,1024,3584]{2,1,0:T(8,128)(2,1)}, u32[]{:S(2)}) copy-start(bf16[1,1024,3584]{2,1,0:T(8,128)(2,1)} %second.1) | copy-start | bytes 22020100
  44.8 31.6 %copy-start.4 = (f32[16,8]{0,1:T(8,128)S(1)}, f32[16,8]{0,1:T(8,128)}, u32[]{:S(2)}) copy-start(f32[16,8]{0,1:T(8,128)} %param.7) | copy-start | bytes 1540

commit v7 on v6

--- a/solution.py
+++ b/solution.py
@@ -15,7 +15,7 @@
 
 
 def column_kernel(sizes, expert_ref):
-    left = lax.broadcasted_iota(jnp.int32, expert_ref.shape, 1) // most
+    left = lax.broadcasted_iota(jnp.int32, expert_ref.shape, 0) // most
     place = {}
     for axis in reversed(turn):
         place[axis] = left % sizes[axis]
@@ -27,32 +27,27 @@
 
 
 def pick_kernel(routes_ref, expert_ref, pick_ref):
-    routes = routes_ref[...].T
     expert = expert_ref[...]
-    rows, top = routes.shape
+    top, rows = routes_ref.shape
     named = jnp.zeros(expert.shape, jnp.float32)
     for k in range(top):
-        named = named + (routes[:, k : k + 1] == expert).astype(jnp.float32)
+        named = jnp.where(routes_ref[k : k + 1, :] == expert, 1.0, named)
     earlier = (
         lax.broadcasted_iota(jnp.int32, (rows, rows), 0)
-        > lax.broadcasted_iota(jnp.int32, (rows, rows), 1)
+        < lax.broadcasted_iota(jnp.int32, (rows, rows), 1)
     ).astype(jnp.float32)
-    position = jnp.dot(earlier, named, preferred_element_type=jnp.float32)
-    slot = (lax.broadcasted_iota(jnp.int32, expert.shape, 1) % most).astype(jnp.float32)
-    filled = (named > 0.5) & (jnp.abs(position - slot) < 0.5)
-    pick_ref[...] = filled.astype(jnp.float32).astype(jnp.bfloat16)
+    position = jnp.dot(
+        named.astype(jnp.bfloat16), earlier.astype(jnp.bfloat16), preferred_element_type=jnp.float32
+    )
+    slot = (lax.broadcasted_iota(jnp.int32, expert.shape, 0) % most).astype(jnp.float32)
+    pick_ref[...] = jnp.where(jnp.abs(position - slot) < 0.5, named, 0.0).astype(jnp.bfloat16)
 
 
 def dispatch_kernel(pick_ref, states_ref, out_ref):
     experts, _, width = out_ref.shape
     tile = 512
     for c in range(0, width, tile):
-        block = lax.dot_general(
-            pick_ref[...],
-            states_ref[:, c : c + tile],
-            (((0,), (0,)), ((), ())),
-            preferred_element_type=jnp.float32,
-        )
+        block = jnp.dot(pick_ref[...], states_ref[:, c : c + tile], preferred_element_type=jnp.float32)
         out_ref[:, :, c : c + tile] = block.astype(jnp.bfloat16).reshape(experts, most, tile)
 
 
@@ -74,19 +69,20 @@
 
 def combine_kernel(routes_ref, scores_ref, pick_ref, expert_ref, states_ref, got_ref, out_ref):
     rows, width = states_ref.shape
-    routes = routes_ref[...].T
-    scores = scores_ref[...].T
+    scores = scores_ref[...]
     expert = expert_ref[...]
     pick = pick_ref[...]
-    weights = scores / jnp.sum(scores, axis=1, keepdims=True) * route_scale
+    weights = scores / jnp.sum(scores, axis=0, keepdims=True) * route_scale
     weight = jnp.zeros(expert.shape, jnp.float32)
-    for k in range(routes.shape[1]):
-        weight = jnp.where(routes[:, k : k + 1] == expert, weights[:, k : k + 1], weight)
+    for k in range(routes_ref.shape[0]):
+        weight = jnp.where(routes_ref[k : k + 1, :] == expert, weights[k : k + 1, :], weight)
     high = weight.astype(jnp.bfloat16)
     low = (weight - high.astype(jnp.float32)).astype(jnp.bfloat16)
-    mix = jnp.concatenate([pick * high, pick * low], axis=0)
-    total = jnp.dot(mix, got_ref[...].reshape(-1, width), preferred_element_type=jnp.float32)
-    out_ref[...] = (states_ref[...].astype(jnp.float32) + (total[:rows] + total[rows:])).astype(jnp.bfloat16)
+    got = got_ref[...].reshape(-1, width)
+    mix = jnp.concatenate([pick * high, pick * low], axis=1)
+    total = lax.dot_general(mix, got, (((0,), (0,)), ((), ())), preferred_element_type=jnp.float32)
+    total = total[:rows] + total[rows:]
+    out_ref[...] = (states_ref[...].astype(jnp.float32) + total).astype(jnp.bfloat16)
 
 
 def body(states, routes, gate_scores, w_in, w_out):
@@ -102,7 +98,7 @@
 
     expert = pl.pallas_call(
         functools.partial(column_kernel, {axis: lax.axis_size(axis) for axis in axes}),
-        out_shape=jax.ShapeDtypeStruct((rows, slots), jnp.int32),
+        out_shape=jax.ShapeDtypeStruct((slots, rows), jnp.int32),
         out_specs=vmem,
         compiler_params=small,
         cost_estimate=pl.CostEstimate(flops=16 * work, bytes_accessed=8 * weights, transcendentals=0),
@@ -110,7 +106,7 @@
     )()
     pick = pl.pallas_call(
         pick_kernel,
-        out_shape=jax.ShapeDtypeStruct((rows, slots), jnp.bfloat16),
+        out_shape=jax.ShapeDtypeStruct((slots, rows), jnp.bfloat16),
         in_specs=[vmem] * 2,
         out_specs=vmem,
         compiler_params=small,

time: 77.9 us -> 77.7 us (level)
  no operation moved by 1% of the time
where the time goes in v7:
time: 77.7 us; the launch traced here: 77.6 us
  blocking collectives  68.9 us (89%)
  Pallas kernels  8.19 us (11%)
    all_to_all x1, blocking collectives, body(): lax.all_to_all(outgoing, turn, split_axis=0, concat_axis=0, tiled=True)  37.3 us
    all_to_all x1, blocking collectives, body(): lax.all_to_all(result, turn, split_axis=0, concat_axis=0, tiled=True)  31.6 us
    pallas_call x1, Pallas kernels, body(): pl.pallas_call(ffn_kernel, out_shape=message, in_specs=[vmem] * 3, out_sp...  5.89 us

profile of v7, /device:TPU:1, one launch (start us, length us, event | category | flops | bytes accessed | tf_op | source)
XLA Modules:
  0.0 77.6 jit_solution(12888072612527928889)
XLA Ops:
  0.0 0.0 copy-start.3
  0.0 0.0 copy-start.2
  0.0 0.0 copy-start
  0.0 0.0 copy-start.1
  0.0 0.2 columns.1.expert_ref
  0.3 0.4 copy-done.3
  0.7 0.2 pick.1.pick_ref
  0.9 0.0 copy-done.2
  0.9 0.6 dispatch.1
  1.5 37.3 %all_to_all.10.in_ref = bf16[128,2,3584]{2,1,0:T(2,128)(2,1)S(1)} all-to-all(bf16[128,2,3584]{2,1,0:T(2,128)(2,1)S(1)} %dispatch.1), channel_id=1, replica_groups=mesh['grp'=2,'x'=4,'y'=4,'z'=4] {'grp','z','y','x'}, dimensions={0} | all-to-all | bytes 3670016 | tf_op jit(solution)/shard_map/all_to_all | solution.py:123
  38.8 0.0 copy-done
  38.8 0.0 copy-done.1
  38.8 5.9 %expert_ffn.1 = bf16[128,2,3584]{2,1,0:T(2,128)(2,1)S(1)} custom-call(bf16[128,2,3584]{2,1,0:T(2,128)(2,1)S(1)} %all_to_all.10.in_ref, bf16[1,3584,2048]{2,1,0:T(8,128)(2,1)S(1)} %copy-done, bf16[1,1024,3584]{2,1,0:T(8,128)(2,1)S(1)} %copy-done.1), custom_call_target="tpu_custom_call" | custom-call | flops 5637144576 | bytes 22020096 | tf_op jit(solution)/shard_map/expert_ffn/pallas_call | solution.py:124
  44.7 0.0 copy-start.4
  44.7 31.6 %all_to_all.11.got_ref = bf16[128,2,3584]{2,1,0:T(2,128)(2,1)S(1)} all-to-all(bf16[128,2,3584]{2,1,0:T(2,128)(2,1)S(1)} %expert_ffn.1), channel_id=1, replica_groups=mesh['grp'=2,'x'=4,'y'=4,'z'=4] {'grp','z','y','x'}, dimensions={0} | all-to-all | bytes 3670016 | tf_op jit(solution)/shard_map/all_to_all | solution.py:139
  76.3 0.0 copy-done.4
  76.3 1.3 %combine.1 = bf16[16,3584]{1,0:T(8,128)(2,1)} custom-call(s32[8,16]{1,0:T(8,128)S(1)} %bitcast.3, f32[8,16]{1,0:T(8,128)S(1)} %bitcast.4, bf16[256,16]{1,0:T(8,128)(2,1)S(1)} %pick.1.pick_ref, s32[256,16]{1,0:T(8,128)S(1)} %columns.1.expert_ref, bf16[16,3584]{1,0:T(8,128)(2,1)S(1)} %copy-done.2, bf16[128,2,3584]{2,1,0:T(2,128)(2,1)S(1)} %all_to_all.11.got_ref), custom_call_target="tpu_custom_call" | custom-call | tf_op jit(solution)/shard_map/combine/pallas_call | solution.py:140
Async XLA Ops:
  0.0 0.7 copy-start.3
  0.0 0.9 %copy-start.2 = (bf16[16,3584]{1,0:T(8,128)(2,1)S(1)}, bf16[16,3584]{1,0:T(8,128)(2,1)}, u32[]{:S(2)}) copy-start(bf16[16,3584]{1,0:T(8,128)(2,1)} %states_ref.3) | copy-start | bytes 344068
  0.0 38.8 %copy-start = (bf16[1,3584,2048]{2,1,0:T(8,128)(2,1)S(1)}, bf16[1,3584,2048]{2,1,0:T(8,128)(2,1)}, u32[]{:S(2)}) copy-start(bf16[1,3584,2048]{2,1,0:T(8,128)(2,1)} %first.1) | copy-start | bytes 44040196
  0.0 38.8 %copy-start.1 = (bf16[1,1024,3584]{2,1,0:T(8,128)(2,1)S(1)}, bf16[1,1024,3584]{2,1,0:T(8,128)(2,1)}, u32[]{:S(2)}) copy-start(bf16[1,1024,3584]{2,1,0:T(8,128)(2,1)} %second.1) | copy-start | bytes 22020100
  44.7 31.6 %copy-start.4 = (f32[16,8]{0,1:T(8,128)S(1)}, f32[16,8]{0,1:T(8,128)}, u32[]{:S(2)}) copy-start(f32[16,8]{0,1:T(8,128)} %param.7) | copy-start | bytes 1540

commit v8 on v7

--- a/solution.py
+++ b/solution.py
@@ -43,12 +43,22 @@
     pick_ref[...] = jnp.where(jnp.abs(position - slot) < 0.5, named, 0.0).astype(jnp.bfloat16)
 
 
-def dispatch_kernel(pick_ref, states_ref, out_ref):
+def dispatch_kernel(pick_ref, states_ref, routes_ref, scores_ref, expert_ref, out_ref, mix_ref):
     experts, _, width = out_ref.shape
+    pick = pick_ref[...]
     tile = 512
     for c in range(0, width, tile):
-        block = jnp.dot(pick_ref[...], states_ref[:, c : c + tile], preferred_element_type=jnp.float32)
+        block = jnp.dot(pick, states_ref[:, c : c + tile], preferred_element_type=jnp.float32)
         out_ref[:, :, c : c + tile] = block.astype(jnp.bfloat16).reshape(experts, most, tile)
+    scores = scores_ref[...]
+    expert = expert_ref[...]
+    weights = scores / jnp.sum(scores, axis=0, keepdims=True) * route_scale
+    weight = jnp.zeros(expert.shape, jnp.float32)
+    for k in range(routes_ref.shape[0]):
+        weight = jnp.where(routes_ref[k : k + 1, :] == expert, weights[k : k + 1, :], weight)
+    high = weight.astype(jnp.bfloat16)
+    low = (weight - high.astype(jnp.float32)).astype(jnp.bfloat16)
+    mix_ref[...] = jnp.concatenate([pick * high, pick * low], axis=1)
 
 
 def ffn_kernel(in_ref, first, second, out_ref, rows_in, hidden):
@@ -67,22 +77,22 @@
         out_ref[:, :, c : c + tile] = block.astype(jnp.bfloat16).reshape(-1, most, tile)
 
 
-def combine_kernel(routes_ref, scores_ref, pick_ref, expert_ref, states_ref, got_ref, out_ref):
+def combine_kernel(mix_ref, states_ref, got_ref, out_hbm, out_ref, sems):
     rows, width = states_ref.shape
-    scores = scores_ref[...]
-    expert = expert_ref[...]
-    pick = pick_ref[...]
-    weights = scores / jnp.sum(scores, axis=0, keepdims=True) * route_scale
-    weight = jnp.zeros(expert.shape, jnp.float32)
-    for k in range(routes_ref.shape[0]):
-        weight = jnp.where(routes_ref[k : k + 1, :] == expert, weights[k : k + 1, :], weight)
-    high = weight.astype(jnp.bfloat16)
-    low = (weight - high.astype(jnp.float32)).astype(jnp.bfloat16)
-    got = got_ref[...].reshape(-1, width)
-    mix = jnp.concatenate([pick * high, pick * low], axis=1)
-    total = lax.dot_general(mix, got, (((0,), (0,)), ((), ())), preferred_element_type=jnp.float32)
-    total = total[:rows] + total[rows:]
-    out_ref[...] = (states_ref[...].astype(jnp.float32) + total).astype(jnp.bfloat16)
+    tile = width // 2
+    copies = []
+    for c in range(0, width, tile):
+        here = pl.ds(c, tile)
+        got = got_ref[:, :, here].reshape(-1, tile)
+        total = lax.dot_general(
+            mix_ref[...], got, (((0,), (0,)), ((), ())), preferred_element_type=jnp.float32
+        )
+        mixed = states_ref[:, here].astype(jnp.float32) + (total[:rows] + total[rows:])
+        out_ref[:, here] = mixed.astype(jnp.bfloat16)
+        copies.append(pltpu.make_async_copy(out_ref.at[:, here], out_hbm.at[:, here], sems.at[c // tile]))
+        copies[-1].start()
+    for copy in copies:
+        copy.wait()
 
 
 def body(states, routes, gate_scores, w_in, w_out):
@@ -112,14 +122,14 @@
         compiler_params=small,
         name="pick",
     )(routes.T, expert)
-    outgoing = pl.pallas_call(
+    outgoing, mix = pl.pallas_call(
         dispatch_kernel,
-        out_shape=message,
-        in_specs=[vmem] * 2,
-        out_specs=vmem,
+        out_shape=[message, jax.ShapeDtypeStruct((slots, 2 * rows), jnp.bfloat16)],
+        in_specs=[vmem] * 5,
+        out_specs=[vmem] * 2,
         compiler_params=small,
         name="dispatch",
-    )(pick, states)
+    )(pick, states, routes.T, gate_scores.T, expert)
     received = lax.all_to_all(outgoing, turn, split_axis=0, concat_axis=0, tiled=True)
     result = pl.pallas_call(
         ffn_kernel,
@@ -140,11 +150,12 @@
     return pl.pallas_call(
         combine_kernel,
         out_shape=jax.ShapeDtypeStruct((rows, width), jnp.bfloat16),
-        in_specs=[vmem] * 6,
-        out_specs=vmem,
+        in_specs=[vmem] * 3,
+        out_specs=pl.BlockSpec(memory_space=pl.ANY),
+        scratch_shapes=[pltpu.VMEM((rows, width), jnp.bfloat16), pltpu.SemaphoreType.DMA((2,))],
         compiler_params=small,
         name="combine",
-    )(routes.T, gate_scores.T, pick, expert, states, returned)
+    )(mix, states, returned)
 
 
 def solution(mesh):

time: 77.7 us -> 77.6 us (level)
  no operation moved by 1% of the time
where the time goes in v8:
time: 77.6 us; the launch traced here: 77.5 us
  blocking collectives  68.9 us (89%)
  Pallas kernels  8.11 us (10%)
    all_to_all x1, blocking collectives, body(): lax.all_to_all(outgoing, turn, split_axis=0, concat_axis=0, tiled=True)  37.3 us
    all_to_all x1, blocking collectives, body(): lax.all_to_all(result, turn, split_axis=0, concat_axis=0, tiled=True)  31.6 us
    pallas_call x1, Pallas kernels, body(): pl.pallas_call(ffn_kernel, out_shape=message, in_specs=[vmem] * 3, out_sp...  5.89 us

profile of v8, /device:TPU:1, one launch (start us, length us, event | category | flops | bytes accessed | tf_op | source)
XLA Modules:
  0.0 77.5 jit_solution(12260051638629895592)
XLA Ops:
  0.0 0.0 copy-start.3
  0.0 0.0 copy-start.2
  0.0 0.0 copy-start.4
  0.0 0.0 copy-start
  0.0 0.0 copy-start.1
  0.0 0.2 columns.1.expert_ref
  0.3 0.4 copy-done.3
  0.7 0.2 pick.1.pick_ref
  0.9 0.0 copy-done.2
  0.9 0.0 copy-done.4
  0.9 0.7 dispatch.1
  1.6 37.3 %all_to_all.10.in_ref = bf16[128,2,3584]{2,1,0:T(2,128)(2,1)S(1)} all-to-all(bf16[128,2,3584]{2,1,0:T(2,128)(2,1)S(1)} %get-tuple-element.8), channel_id=1, replica_groups=mesh['grp'=2,'x'=4,'y'=4,'z'=4] {'grp','z','y','x'}, dimensions={0} | all-to-all | bytes 3670016 | tf_op jit(solution)/shard_map/all_to_all | solution.py:133
  38.9 0.0 copy-done
  38.9 0.0 copy-done.1
  38.9 5.9 %expert_ffn.1 = bf16[128,2,3584]{2,1,0:T(2,128)(2,1)S(1)} custom-call(bf16[128,2,3584]{2,1,0:T(2,128)(2,1)S(1)} %all_to_all.10.in_ref, bf16[1,3584,2048]{2,1,0:T(8,128)(2,1)S(1)} %copy-done, bf16[1,1024,3584]{2,1,0:T(8,128)(2,1)S(1)} %copy-done.1), custom_call_target="tpu_custom_call" | custom-call | flops 5637144576 | bytes 22020096 | tf_op jit(solution)/shard_map/expert_ffn/pallas_call | solution.py:134
  44.8 31.6 %all_to_all.11.got_ref = bf16[128,2,3584]{2,1,0:T(2,128)(2,1)S(1)} all-to-all(bf16[128,2,3584]{2,1,0:T(2,128)(2,1)S(1)} %expert_ffn.1), channel_id=1, replica_groups=mesh['grp'=2,'x'=4,'y'=4,'z'=4] {'grp','z','y','x'}, dimensions={0} | all-to-all | bytes 3670016 | tf_op jit(solution)/shard_map/all_to_all | solution.py:149
  76.4 1.1 %combine.1 = bf16[16,3584]{1,0:T(8,128)(2,1)} custom-call(bf16[256,32]{1,0:T(8,128)(2,1)S(1)} %get-tuple-element.7.mix_ref, bf16[16,3584]{1,0:T(8,128)(2,1)S(1)} %copy-done.2, bf16[128,2,3584]{2,1,0:T(2,128)(2,1)S(1)} %all_to_all.11.got_ref), custom_call_target="tpu_custom_call" | custom-call | tf_op jit(solution)/shard_map/combine/pallas_call | solution.py:150
Async XLA Ops:
  0.0 0.7 copy-start.3
  0.0 0.9 %copy-start.2 = (bf16[16,3584]{1,0:T(8,128)(2,1)S(1)}, bf16[16,3584]{1,0:T(8,128)(2,1)}, u32[]{:S(2)}) copy-start(bf16[16,3584]{1,0:T(8,128)(2,1)} %states_ref.3) | copy-start | bytes 344068
  0.0 0.9 %copy-start.4 = (f32[16,8]{0,1:T(8,128)S(1)}, f32[16,8]{0,1:T(8,128)}, u32[]{:S(2)}) copy-start(f32[16,8]{0,1:T(8,128)} %param.7) | copy-start | bytes 1540
  0.0 38.9 %copy-start = (bf16[1,3584,2048]{2,1,0:T(8,128)(2,1)S(1)}, bf16[1,3584,2048]{2,1,0:T(8,128)(2,1)}, u32[]{:S(2)}) copy-start(bf16[1,3584,2048]{2,1,0:T(8,128)(2,1)} %first.1) | copy-start | bytes 44040196
  0.0 38.9 %copy-start.1 = (bf16[1,1024,3584]{2,1,0:T(8,128)(2,1)S(1)}, bf16[1,1024,3584]{2,1,0:T(8,128)(2,1)}, u32[]{:S(2)}) copy-start(bf16[1,1024,3584]{2,1,0:T(8,128)(2,1)} %second.1) | copy-start | bytes 22020100

commit v9 on v8

--- a/solution.py
+++ b/solution.py
@@ -46,10 +46,6 @@
 def dispatch_kernel(pick_ref, states_ref, routes_ref, scores_ref, expert_ref, out_ref, mix_ref):
     experts, _, width = out_ref.shape
     pick = pick_ref[...]
-    tile = 512
-    for c in range(0, width, tile):
-        block = jnp.dot(pick, states_ref[:, c : c + tile], preferred_element_type=jnp.float32)
-        out_ref[:, :, c : c + tile] = block.astype(jnp.bfloat16).reshape(experts, most, tile)
     scores = scores_ref[...]
     expert = expert_ref[...]
     weights = scores / jnp.sum(scores, axis=0, keepdims=True) * route_scale
@@ -59,6 +55,10 @@
     high = weight.astype(jnp.bfloat16)
     low = (weight - high.astype(jnp.float32)).astype(jnp.bfloat16)
     mix_ref[...] = jnp.concatenate([pick * high, pick * low], axis=1)
+    tile = 512
+    for c in range(0, width, tile):
+        block = jnp.dot(pick, states_ref[:, c : c + tile], preferred_element_type=jnp.float32)
+        out_ref[:, :, c : c + tile] = block.astype(jnp.bfloat16).reshape(experts, most, tile)
 
 
 def ffn_kernel(in_ref, first, second, out_ref, rows_in, hidden):
@@ -79,7 +79,7 @@
 
 def combine_kernel(mix_ref, states_ref, got_ref, out_hbm, out_ref, sems):
     rows, width = states_ref.shape
-    tile = width // 2
+    tile = width // 4
     copies = []
     for c in range(0, width, tile):
         here = pl.ds(c, tile)
@@ -152,7 +152,7 @@
         out_shape=jax.ShapeDtypeStruct((rows, width), jnp.bfloat16),
         in_specs=[vmem] * 3,
         out_specs=pl.BlockSpec(memory_space=pl.ANY),
-        scratch_shapes=[pltpu.VMEM((rows, width), jnp.bfloat16), pltpu.SemaphoreType.DMA((2,))],
+        scratch_shapes=[pltpu.VMEM((rows, width), jnp.bfloat16), pltpu.SemaphoreType.DMA((4,))],
         compiler_params=small,
         name="combine",
     )(mix, states, returned)

time: 77.6 us -> 77.6 us (level)
  no operation moved by 1% of the time
where the time goes in v9:
time: 77.6 us; the launch traced here: 77.5 us
  blocking collectives  68.9 us (89%)
  Pallas kernels  8.09 us (10%)
    all_to_all x1, blocking collectives, body(): lax.all_to_all(outgoing, turn, split_axis=0, concat_axis=0, tiled=True)  37.3 us
    all_to_all x1, blocking collectives, body(): lax.all_to_all(result, turn, split_axis=0, concat_axis=0, tiled=True)  31.6 us
    pallas_call x1, Pallas kernels, body(): pl.pallas_call(ffn_kernel, out_shape=message, in_specs=[vmem] * 3, out_sp...  5.89 us

profile of v9, /device:TPU:1, one launch (start us, length us, event | category | flops | bytes accessed | tf_op | source)
XLA Modules:
  0.0 77.5 jit_solution(8827653415144817332)
XLA Ops:
  0.0 0.0 copy-start.3
  0.0 0.0 copy-start.2
  0.0 0.0 copy-start.4
  0.0 0.0 copy-start
  0.0 0.0 copy-start.1
  0.0 0.2 columns.1.expert_ref
  0.3 0.4 copy-done.3
  0.7 0.2 pick.1.pick_ref
  0.9 0.0 copy-done.2
  0.9 0.0 copy-done.4
  0.9 0.7 dispatch.1
  1.6 37.3 %all_to_all.10.in_ref = bf16[128,2,3584]{2,1,0:T(2,128)(2,1)S(1)} all-to-all(bf16[128,2,3584]{2,1,0:T(2,128)(2,1)S(1)} %get-tuple-element.8), channel_id=1, replica_groups=mesh['grp'=2,'x'=4,'y'=4,'z'=4] {'grp','z','y','x'}, dimensions={0} | all-to-all | bytes 3670016 | tf_op jit(solution)/shard_map/all_to_all | solution.py:133
  38.9 0.0 copy-done
  38.9 0.0 copy-done.1
  38.9 5.9 %expert_ffn.1 = bf16[128,2,3584]{2,1,0:T(2,128)(2,1)S(1)} custom-call(bf16[128,2,3584]{2,1,0:T(2,128)(2,1)S(1)} %all_to_all.10.in_ref, bf16[1,3584,2048]{2,1,0:T(8,128)(2,1)S(1)} %copy-done, bf16[1,1024,3584]{2,1,0:T(8,128)(2,1)S(1)} %copy-done.1), custom_call_target="tpu_custom_call" | custom-call | flops 5637144576 | bytes 22020096 | tf_op jit(solution)/shard_map/expert_ffn/pallas_call | solution.py:134
  44.8 31.6 %all_to_all.11.got_ref = bf16[128,2,3584]{2,1,0:T(2,128)(2,1)S(1)} all-to-all(bf16[128,2,3584]{2,1,0:T(2,128)(2,1)S(1)} %expert_ffn.1), channel_id=1, replica_groups=mesh['grp'=2,'x'=4,'y'=4,'z'=4] {'grp','z','y','x'}, dimensions={0} | all-to-all | bytes 3670016 | tf_op jit(solution)/shard_map/all_to_all | solution.py:149
  76.4 1.1 %combine.1 = bf16[16,3584]{1,0:T(8,128)(2,1)} custom-call(bf16[256,32]{1,0:T(8,128)(2,1)S(1)} %get-tuple-element.7.mix_ref, bf16[16,3584]{1,0:T(8,128)(2,1)S(1)} %copy-done.2, bf16[128,2,3584]{2,1,0:T(2,128)(2,1)S(1)} %all_to_all.11.got_ref), custom_call_target="tpu_custom_call" | custom-call | tf_op jit(solution)/shard_map/combine/pallas_call | solution.py:150
Async XLA Ops:
  0.0 0.7 copy-start.3
  0.0 0.9 %copy-start.2 = (bf16[16,3584]{1,0:T(8,128)(2,1)S(1)}, bf16[16,3584]{1,0:T(8,128)(2,1)}, u32[]{:S(2)}) copy-start(bf16[16,3584]{1,0:T(8,128)(2,1)} %states_ref.3) | copy-start | bytes 344068
  0.0 0.9 %copy-start.4 = (f32[16,8]{0,1:T(8,128)S(1)}, f32[16,8]{0,1:T(8,128)}, u32[]{:S(2)}) copy-start(f32[16,8]{0,1:T(8,128)} %param.7) | copy-start | bytes 1540
  0.0 38.9 %copy-start = (bf16[1,3584,2048]{2,1,0:T(8,128)(2,1)S(1)}, bf16[1,3584,2048]{2,1,0:T(8,128)(2,1)}, u32[]{:S(2)}) copy-start(bf16[1,3584,2048]{2,1,0:T(8,128)(2,1)} %first.1) | copy-start | bytes 44040196
  0.0 38.9 %copy-start.1 = (bf16[1,1024,3584]{2,1,0:T(8,128)(2,1)S(1)}, bf16[1,1024,3584]{2,1,0:T(8,128)(2,1)}, u32[]{:S(2)}) copy-start(bf16[1,1024,3584]{2,1,0:T(8,128)(2,1)} %second.1) | copy-start | bytes 22020100

commit v10 on v9

--- a/solution.py
+++ b/solution.py
@@ -55,7 +55,7 @@
     high = weight.astype(jnp.bfloat16)
     low = (weight - high.astype(jnp.float32)).astype(jnp.bfloat16)
     mix_ref[...] = jnp.concatenate([pick * high, pick * low], axis=1)
-    tile = 512
+    tile = width // 2
     for c in range(0, width, tile):
         block = jnp.dot(pick, states_ref[:, c : c + tile], preferred_element_type=jnp.float32)
         out_ref[:, :, c : c + tile] = block.astype(jnp.bfloat16).reshape(experts, most, tile)

time: 77.6 us -> 77.7 us (level)
  no operation moved by 1% of the time
where the time goes in v10:
time: 77.7 us; the launch traced here: 77.5 us
  blocking collectives  68.9 us (89%)
  Pallas kernels  8.14 us (10%)
    all_to_all x1, blocking collectives, body(): lax.all_to_all(outgoing, turn, split_axis=0, concat_axis=0, tiled=True)  37.3 us
    all_to_all x1, blocking collectives, body(): lax.all_to_all(result, turn, split_axis=0, concat_axis=0, tiled=True)  31.6 us
    pallas_call x1, Pallas kernels, body(): pl.pallas_call(ffn_kernel, out_shape=message, in_specs=[vmem] * 3, out_sp...  5.9 us

profile of v10, /device:TPU:1, one launch (start us, length us, event | category | flops | bytes accessed | tf_op | source)
XLA Modules:
  0.0 77.5 jit_solution(10639771912751762932)
XLA Ops:
  0.0 0.0 copy-start.3
  0.0 0.0 copy-start.2
  0.0 0.0 copy-start.4
  0.0 0.0 copy-start
  0.0 0.0 copy-start.1
  0.0 0.2 columns.1.expert_ref
  0.3 0.4 copy-done.3
  0.7 0.2 pick.1.pick_ref
  0.9 0.0 copy-done.2
  0.9 0.0 copy-done.4
  0.9 0.7 dispatch.1
  1.7 37.3 %all_to_all.10.in_ref = bf16[128,2,3584]{2,1,0:T(2,128)(2,1)S(1)} all-to-all(bf16[128,2,3584]{2,1,0:T(2,128)(2,1)S(1)} %get-tuple-element.8), channel_id=1, replica_groups=mesh['grp'=2,'x'=4,'y'=4,'z'=4] {'grp','z','y','x'}, dimensions={0} | all-to-all | bytes 3670016 | tf_op jit(solution)/shard_map/all_to_all | solution.py:133
  38.9 0.0 copy-done
  38.9 0.0 copy-done.1
  38.9 5.9 %expert_ffn.1 = bf16[128,2,3584]{2,1,0:T(2,128)(2,1)S(1)} custom-call(bf16[128,2,3584]{2,1,0:T(2,128)(2,1)S(1)} %all_to_all.10.in_ref, bf16[1,3584,2048]{2,1,0:T(8,128)(2,1)S(1)} %copy-done, bf16[1,1024,3584]{2,1,0:T(8,128)(2,1)S(1)} %copy-done.1), custom_call_target="tpu_custom_call" | custom-call | flops 5637144576 | bytes 22020096 | tf_op jit(solution)/shard_map/expert_ffn/pallas_call | solution.py:134
  44.8 31.6 %all_to_all.11.got_ref = bf16[128,2,3584]{2,1,0:T(2,128)(2,1)S(1)} all-to-all(bf16[128,2,3584]{2,1,0:T(2,128)(2,1)S(1)} %expert_ffn.1), channel_id=1, replica_groups=mesh['grp'=2,'x'=4,'y'=4,'z'=4] {'grp','z','y','x'}, dimensions={0} | all-to-all | bytes 3670016 | tf_op jit(solution)/shard_map/all_to_all | solution.py:149
  76.4 1.1 %combine.1 = bf16[16,3584]{1,0:T(8,128)(2,1)} custom-call(bf16[256,32]{1,0:T(8,128)(2,1)S(1)} %get-tuple-element.7.mix_ref, bf16[16,3584]{1,0:T(8,128)(2,1)S(1)} %copy-done.2, bf16[128,2,3584]{2,1,0:T(2,128)(2,1)S(1)} %all_to_all.11.got_ref), custom_call_target="tpu_custom_call" | custom-call | tf_op jit(solution)/shard_map/combine/pallas_call | solution.py:150
Async XLA Ops:
  0.0 0.7 copy-start.3
  0.0 0.9 %copy-start.2 = (bf16[16,3584]{1,0:T(8,128)(2,1)S(1)}, bf16[16,3584]{1,0:T(8,128)(2,1)}, u32[]{:S(2)}) copy-start(bf16[16,3584]{1,0:T(8,128)(2,1)} %states_ref.3) | copy-start | bytes 344068
  0.0 0.9 %copy-start.4 = (f32[16,8]{0,1:T(8,128)S(1)}, f32[16,8]{0,1:T(8,128)}, u32[]{:S(2)}) copy-start(f32[16,8]{0,1:T(8,128)} %param.7) | copy-start | bytes 1540
  0.0 38.9 %copy-start = (bf16[1,3584,2048]{2,1,0:T(8,128)(2,1)S(1)}, bf16[1,3584,2048]{2,1,0:T(8,128)(2,1)}, u32[]{:S(2)}) copy-start(bf16[1,3584,2048]{2,1,0:T(8,128)(2,1)} %first.1) | copy-start | bytes 44040196
  0.0 38.9 %copy-start.1 = (bf16[1,1024,3584]{2,1,0:T(8,128)(2,1)S(1)}, bf16[1,1024,3584]{2,1,0:T(8,128)(2,1)}, u32[]{:S(2)}) copy-start(bf16[1,1024,3584]{2,1,0:T(8,128)(2,1)} %second.1) | copy-start | bytes 22020100
